TPU v7x, 256 devices: a whole 4x4x8 slice. The times are simulated.
256 devices in a mesh: img: 64 (over z, x, core), rep: 4 (over y).
Axes of the slice: x: 4, y: 4, z: 8, core: 2. Of those that a mesh axis runs over, the one named last changes fastest.
Arguments:
- tokens: bfloat16 [512, 24, 1024], P('img'), may hold values from -6 to 6
- proj_in: bfloat16 [1024, 768], replicated, may hold values from -0.1875 to 0.1875
- attn_query: bfloat16 [768, 768], replicated, may hold values from -1 to 1
- attn_keyval: bfloat16 [768, 1536], replicated, may hold values from -1 to 1
- attn_output: bfloat16 [768, 768], replicated, may hold values from -0.21875 to 0.21875
- mlp_up: bfloat16 [768, 1536], replicated, may hold values from -0.21875 to 0.21875
- mlp_down: bfloat16 [1536, 768], replicated, may hold values from -0.15625 to 0.15625
- pair_list: int32 [8192, 2], P(('img', 'rep')), may hold values from 0 to 511, as said below
- conf_level: int32 [8192], P(('img', 'rep')), may hold values from 0 to 15
- conf_table: float32 [16], replicated, may hold values from 0.1 to 1
Outputs:
- joined: bfloat16 [512, 24, 768], P('img')
Inputs may be any that keep to these rules, and one draw needn't show every extreme that they name: `pair_list`: the two images of a pair differ. Among the 64 image entries of the pairs of one device, at most 2 lie in the images o * 8 to (o + 1) * 8 - 1 of one index o of img, and on every device some o has exactly 2.
All inputs are finite; a program needn't handle non-finite values.
Results may differ from a plain program's by a relative error of at most 0.014.
Values may be sent and summed in bfloat16 or wider, within the bound.
A program may use at most 128 MiB of HBM per device.

v0:
```python
import jax
import jax.numpy as jnp
from jax import lax
from jax.sharding import PartitionSpec as P

HEAD_DIM = 64
CAP = 2


def normalize(values):
    centred = values - jnp.mean(values, axis=-1, keepdims=True)
    spread = jnp.mean(centred * centred, axis=-1, keepdims=True)
    return centred * lax.rsqrt(spread + 1e-06)


def attend(query_side, memory_side, query_weight, keyval_weight, output_weight):
    pair_count, tok_count, model_width = query_side.shape
    head_count = model_width // HEAD_DIM
    query_norm = (
        normalize(query_side.astype(jnp.float32)).astype(jnp.bfloat16).reshape(-1, model_width)
    )
    memory_norm = (
        normalize(memory_side.astype(jnp.float32)).astype(jnp.bfloat16).reshape(-1, model_width)
    )
    queries = jnp.dot(query_norm, query_weight, preferred_element_type=jnp.float32).astype(
        jnp.bfloat16
    )
    queries = queries.reshape(pair_count, tok_count, head_count, HEAD_DIM)
    keyvals = jnp.dot(memory_norm, keyval_weight, preferred_element_type=jnp.float32).astype(
        jnp.bfloat16
    )
    keyvals = keyvals.reshape(pair_count, tok_count, 2, head_count, HEAD_DIM)
    scores = jnp.einsum(
        "bqhd,bkhd->bhqk", queries, keyvals[:, :, 0], preferred_element_type=jnp.float32
    )
    scores = scores / jnp.sqrt(jnp.float32(HEAD_DIM))
    scores = scores - jnp.max(scores, axis=-1, keepdims=True)
    expd = jnp.exp(scores)
    attention = (expd / jnp.sum(expd, axis=-1, keepdims=True)).astype(jnp.bfloat16)
    attended = jnp.einsum(
        "bhqk,bkhd->bqhd", attention, keyvals[:, :, 1], preferred_element_type=jnp.float32
    )
    attended = attended.astype(jnp.bfloat16).reshape(-1, model_width)
    return query_side.astype(jnp.float32).reshape(-1, model_width) + jnp.dot(
        attended, output_weight, preferred_element_type=jnp.float32
    )


def body(
    tokens,
    proj_in,
    attn_query,
    attn_keyval,
    attn_output,
    mlp_up,
    mlp_down,
    pair_list,
    conf_level,
    conf_table,
):
    img_dev, tok_count, enc_width = tokens.shape
    model_width = attn_query.shape[0]
    peer_count = lax.axis_size("img")
    pair_count = pair_list.shape[0]
    end_count = 2 * pair_count
    slot_total = peer_count * CAP
    endpoints = jnp.concatenate([pair_list[:, 0], pair_list[:, 1]])
    owner_idx = endpoints // img_dev
    same_owner = owner_idx[:, None] == owner_idx[None, :]
    positions = jnp.arange(end_count, dtype=jnp.int32)
    earlier = positions[:, None] > positions[None, :]
    slot_rank = jnp.sum((same_owner & earlier).astype(jnp.int32), axis=1)
    slot_idx = owner_idx * CAP + slot_rank
    slot_hit = slot_idx[:, None] == jnp.arange(slot_total, dtype=jnp.int32)[None, :]
    request = jnp.max(jnp.where(slot_hit, (endpoints % img_dev)[:, None], -1), axis=0).reshape(
        peer_count, CAP
    )
    received = lax.all_to_all(request, "img", split_axis=0, concat_axis=0, tiled=True)
    row_idx = jnp.maximum(received, 0).reshape(-1)
    reply_rows = tokens[row_idx].reshape(peer_count, CAP, tok_count, enc_width)
    arrived = lax.all_to_all(reply_rows, "img", split_axis=0, concat_axis=0, tiled=True).reshape(
        slot_total, tok_count, enc_width
    )
    picked = arrived[slot_idx].reshape(-1, enc_width)
    gathered = jnp.dot(picked, proj_in, preferred_element_type=jnp.float32)
    gathered = gathered.astype(jnp.bfloat16).reshape(end_count, tok_count, model_width)
    hidden = attend(
        gathered[:pair_count], gathered[pair_count:], attn_query, attn_keyval, attn_output
    )
    hidden_norm = normalize(hidden).astype(jnp.bfloat16)
    expanded = jax.nn.gelu(
        jnp.dot(hidden_norm, mlp_up, preferred_element_type=jnp.float32), approximate=False
    )
    output = hidden + jnp.dot(
        expanded.astype(jnp.bfloat16), mlp_down, preferred_element_type=jnp.float32
    )
    level_hit = conf_level[:, None] == jnp.arange(conf_table.shape[0], dtype=jnp.int32)[None, :]
    confidence = jnp.sum(jnp.where(level_hit, conf_table[None, :], 0.0), axis=1)
    features = (
        confidence[:, None, None] * output.reshape(pair_count, tok_count, model_width)
    ).astype(jnp.bfloat16)
    both_sides = jnp.concatenate([features, features], axis=0)
    outgoing = (
        jnp.zeros((slot_total, tok_count, model_width), jnp.bfloat16).at[slot_idx].set(both_sides)
    )
    outgoing = outgoing.reshape(peer_count, CAP, tok_count, model_width)
    returned = lax.all_to_all(outgoing, "img", split_axis=0, concat_axis=0, tiled=True).reshape(
        slot_total, tok_count * model_width
    )
    target = (
        received.reshape(-1)[:, None] == jnp.arange(img_dev, dtype=jnp.int32)[None, :]
    ).astype(jnp.bfloat16)
    partial_sums = jnp.dot(target.T, returned, preferred_element_type=jnp.float32)
    partial_sums = partial_sums.reshape(img_dev, tok_count, model_width)
    image_sums = lax.psum(partial_sums.astype(jnp.bfloat16), "rep")
    return image_sums


def solution(mesh):
    placed = (
        P("img", None, None),
        P(),
        P(),
        P(),
        P(),
        P(),
        P(),
        P(("img", "rep"), None),
        P(("img", "rep")),
        P(),
    )
    return jax.shard_map(
        body, mesh=mesh, in_specs=placed, out_specs=P("img", None, None), check_vma=False
    )
```

profile of v0, /device:TPU:1, one launch (start us, length us, event | category | flops | bytes accessed | tf_op | source)
XLA Modules:
  0.0 454.3 jit_solution(636189450745876080)
XLA Ops:
  6.5 0.0 copy-start
  6.5 0.8 fusion.83
  7.4 0.1 and_select_fusion.1
  7.5 0.1 and_select_fusion.2
  7.6 0.2 convert_reduce_fusion.2
  7.7 0.1 select_reduce_fusion
  7.8 0.1 all_to_all.12
  8.0 22.2 %all_to_all.19 = s32[64,1,2]{2,1,0:T(1,128)S(1)} all-to-all(s32[64,1,2]{2,1,0:T(1,128)S(1)} %bitcast.50), channel_id=1, replica_groups=mesh['img'=64,'rep'=4] {'img'}, dimensions={0} | all-to-all | bytes 1024 | tf_op jit(solution)/shard_map/all_to_all | solution.py:78
  30.2 0.6 broadcast.295
  30.7 1.4 fusion.81
  32.2 0.1 reshape.457
  32.3 4.6 %gather_fusion = bf16[128,24,1024]{2,1,0:T(8,128)(2,1)} fusion(bf16[8,24,1024]{2,1,0:T(8,128)(2,1)} %param.10, s32[1024]{0:T(1024)S(1)} %pad_clamp_fusion.1), kind=kCustom, calls=%fused_computation | custom fusion | bytes 12583424 | tf_op jit(solution)/shard_map/gather | solution.py:80
  36.9 0.0 copy-start.8
  36.9 0.0 copy-start.9
  36.9 5.9 %all-to-all-start.1 = ((bf16[64,2,24,1024]{3,2,1,0:T(8,128)(2,1)}), bf16[64,2,24,1024]{3,2,1,0:T(8,128)(2,1)}, u32[]{:S(2)}, u32[]{:S(2)}) async-start(bf16[64,2,24,1024]{3,2,1,0:T(8,128)(2,1)} %bitcast.45), calls=%async_computation.1 | async-start | bytes 12582912 | tf_op jit(solution)/shard_map/all_to_all | solution.py:81
  42.8 0.1 fusion.49
  42.9 0.0 copy-done.8
  42.9 0.0 copy-done.9
  42.9 0.1 select_reduce_fusion.1
  43.0 138.6 %all-to-all-done.1 = bf16[64,2,24,1024]{3,2,1,0:T(8,128)(2,1)} async-done(((bf16[64,2,24,1024]{3,2,1,0:T(8,128)(2,1)}), bf16[64,2,24,1024]{3,2,1,0:T(8,128)(2,1)}, u32[]{:S(2)}, u32[]{:S(2)}) %all-to-all-start.1) | async-done | bytes 6291488 | tf_op jit(solution)/shard_map/all_to_all | solution.py:81
  181.6 5.2 %gather_fusion.1 = bf16[64,24,1024]{2,1,0:T(8,128)(2,1)} fusion(bf16[128,24,1024]{2,1,0:T(8,128)(2,1)} %bitcast.7, s32[1024]{0:T(1024)S(1)} %pad_clamp_fusion), kind=kCustom, calls=%fused_computation.1 | custom fusion | bytes 6291712 | tf_op jit(solution)/shard_map/gather | solution.py:84
  186.9 5.0 %convolution_convert_fusion = bf16[1536,768]{1,0:T(8,128)(2,1)S(1)} fusion(bf16[1536,1024]{1,0:T(8,128)(2,1)} %bitcast.48, bf16[1024,768]{1,0:T(8,128)(2,1)} %param.11), kind=kOutput, calls=%fused_computation.30 | convolution fusion | flops 2417098752 | bytes 7077888 | tf_op jit(solution)/shard_map/dot_general | solution.py:85
  191.8 0.0 copy-start.3
  191.9 0.0 copy-start.7
  191.9 0.4 convert_reduce_fusion
  192.3 0.9 fusion.18
  193.1 0.1 copy-done.3
  193.2 0.7 copy-done.7
  194.0 1.2 convolution_convert_fusion.2
  195.1 3.3 reshape.450
  198.5 0.0 copy-done
  198.5 4.9 %convolution_convert_fusion.1 = bf16[768,1536]{1,0:T(8,128)(2,1)} fusion(bf16[768,1536]{1,0:T(8,128)(2,1)S(1)} %copy-done, f32[768]{0:T(1024)S(1)} %add_rsqrt_fusion.2, f32[768]{0:T(1024)S(1)} %get-tuple-element.24, bf16[1536,768]{1,0:T(8,128)(2,1)} %copy-done.3), kind=kOutput, calls=%fused_computation.31 | convolution fusion | flops 1815478272 | bytes 5904384 | tf_op jit(solution)/shard_map/dot_general | solution.py:29
  203.3 8.9 %reshape.449 = bf16[32,24,2,12,64]{4,3,2,1,0:T(8,128)(2,1)} reshape(bf16[768,1536]{1,0:T(8,128)(2,1)} %convolution_convert_fusion.1) | data formatting | bytes 4718592 | tf_op jit(solution)/shard_map/reshape | solution.py:32
  212.2 4.1 fusion.82
  216.3 0.0 copy-done.2
  216.3 1.4 fusion.23
  217.7 12.9 %fusion.84 = (f32[32,12,24]{2,1,0:T(8,128)S(1)}, f32[32,12,24,24]{2,3,1,0:T(8,128)S(1)}) fusion(f32[32,12,24,24]{2,3,1,0:T(8,128)S(1)} %fusion.23), kind=kOutput, calls=%fused_computation.137 | output fusion | flops 884759 | bytes 1806336 | tf_op jit(solution)/shard_map/sub | solution.py:37
  230.6 1.7 convert_bitcast_fusion
  232.3 2.4 copy.36
  234.7 0.0 copy-start.4
  234.7 4.2 reshape.451
  239.0 0.0 copy-done.4
  239.0 2.5 fusion.85
  241.4 0.0 copy-start.5
  241.4 1.4 copy-done.5
  242.8 0.4 multiply_reduce_fusion.1
  243.3 16.6 %fusion.29 = f32[768,768]{1,0:T(8,128)S(1)} fusion(f32[768,768]{1,0:T(8,128)} %copy-done.5, bf16[1536,768]{1,0:T(8,128)(2,1)} %param.16, bf16[768,1536]{1,0:T(8,128)(2,1)} %param.15, f32[768]{0:T(1024)S(1)} %add_rsqrt_fusion, f32[768]{0:T(1024)S(1)} %broadcast_multiply_fusion), kind=kOutput, calls=%fused_computation.55 | convolution fusion | flops 3702915072 | bytes 9443328 | tf_op jit(solution)/shard_map/dot_general | solution.py:94
  259.9 0.2 multiply_convert_fusion
  260.1 0.2 pad_maximum_fusion
  260.3 2.5 broadcast_in_dim.24
  262.8 8.9 %scatter_fusion = bf16[128,24,768]{2,1,0:T(8,128)(2,1)} fusion(bf16[128,24,768]{2,1,0:T(8,128)(2,1)} %broadcast_in_dim.24, s32[64]{0:T(128)S(1)} %fusion.49, bf16[64,24,768]{2,1,0:T(8,128)(2,1)S(1)} %pad_maximum_fusion), kind=kCustom, calls=%fused_computation.2 | custom fusion | bytes 7078144 | tf_op jit(solution)/shard_map/scatter | solution.py:104
  271.7 0.0 copy-start.6
  271.7 8.4 %all-to-all-start.2 = ((bf16[64,2,24,768]{3,2,1,0:T(8,128)(2,1)}), bf16[64,2,24,768]{3,2,1,0:T(8,128)(2,1)}, u32[]{:S(2)}, u32[]{:S(2)}) async-start(bf16[64,2,24,768]{3,2,1,0:T(8,128)(2,1)} %bitcast.44), calls=%async_computation.2 | async-start | bytes 9437184 | tf_op jit(solution)/shard_map/all_to_all | solution.py:107
  280.1 0.0 all-reduce.2.cloned.1.call-start
  280.2 0.0 copy-done.6
  280.2 0.1 eq.62
  280.3 105.1 %all-to-all-done.2 = bf16[64,2,24,768]{3,2,1,0:T(8,128)(2,1)} async-done(((bf16[64,2,24,768]{3,2,1,0:T(8,128)(2,1)}), bf16[64,2,24,768]{3,2,1,0:T(8,128)(2,1)}, u32[]{:S(2)}, u32[]{:S(2)}) %all-to-all-start.2) | async-done | bytes 4718624 | tf_op jit(solution)/shard_map/all_to_all | solution.py:107
  385.4 5.7 %copy.42 = bf16[16,8,24,768]{3,1,2,0:T(8,128)(2,1)} copy(bf16[16,8,24,768]{3,2,1,0:T(8,128)(2,1)} %bitcast.17) | data formatting | bytes 9437184
  391.1 6.8 %copy.37 = bf16[18432,128]{1,0:T(8,128)(2,1)} copy(bf16[18432,128]{0,1:T(8,128)(2,1)} %bitcast.47) | data formatting | bytes 9437184 | tf_op jit(solution)/shard_map/dot_general | solution.py:113
  397.9 4.4 convolution_convert_fusion.3
  402.3 0.0 all-reduce.2.cloned.1.call-update
  402.3 43.4 %all-reduce.2.cloned.1.call-done = bf16[8,24,768]{2,0,1:T(8,128)(2,1)} async-done(((bf16[8,24,768]{2,0,1:T(8,128)(2,1)}), bf16[8,24,768]{2,0,1:T(8,128)(2,1)}) %all-reduce.2.cloned.1.call-update) | async-done | bytes 294928 | tf_op jit(solution)/shard_map/psum | solution.py:115
  445.7 1.7 copy.38
  447.4 0.0 copy-done.1
  (10 shorter events, 0.0 us)
Async XLA Ops:
  6.5 191.9 %copy-start = (bf16[768,1536]{1,0:T(8,128)(2,1)S(1)}, bf16[768,1536]{1,0:T(8,128)(2,1)}, u32[]{:S(2)}) copy-start(bf16[768,1536]{1,0:T(8,128)(2,1)} %param.13) | copy-start | bytes 7077892
  36.9 6.0 %copy-start.8 = (f32[16]{0:T(128)S(1)}, f32[16]{0:T(128)}, u32[]{:S(2)}) copy-start(f32[16]{0:T(128)} %param.19) | copy-start | bytes 196
  36.9 6.0 %copy-start.9 = (s32[32]{0:T(128)S(1)}, s32[32]{0:T(128)}, u32[]{:S(2)}) copy-start(s32[32]{0:T(128)} %param.18) | copy-start | bytes 388
  36.9 144.7 %all-to-all-start.1 = ((bf16[64,2,24,1024]{3,2,1,0:T(8,128)(2,1)}), bf16[64,2,24,1024]{3,2,1,0:T(8,128)(2,1)}, u32[]{:S(2)}, u32[]{:S(2)}) async-start(bf16[64,2,24,1024]{3,2,1,0:T(8,128)(2,1)} %bitcast.45), calls=%async_computation.1 | async-start | bytes 12582912 | tf_op jit(solution)/shard_map/all_to_all | solution.py:81
  191.8 1.4 copy-start.3
  191.9 2.1 copy-start.7
  212.2 4.1 copy-start.2
  234.7 4.2 copy-start.4
  241.4 1.4 copy-start.5
  271.7 8.5 %copy-start.6 = (s32[64,2]{1,0:T(8,128)S(1)}, s32[64,2]{1,0:T(8,128)}, u32[]{:S(2)}) copy-start(s32[64,2]{1,0:T(8,128)} %get-tuple-element.9) | copy-start | bytes 1540
  271.7 113.7 %all-to-all-start.2 = ((bf16[64,2,24,768]{3,2,1,0:T(8,128)(2,1)}), bf16[64,2,24,768]{3,2,1,0:T(8,128)(2,1)}, u32[]{:S(2)}, u32[]{:S(2)}) async-start(bf16[64,2,24,768]{3,2,1,0:T(8,128)(2,1)} %bitcast.44), calls=%async_computation.2 | async-start | bytes 9437184 | tf_op jit(solution)/shard_map/all_to_all | solution.py:107
  280.1 165.6 %all-reduce.2.cloned.1.call-start = ((), (), s32[]{:S(2)}) async-start(), calls=%async_computation.3 | async-start | bytes 589824 | tf_op jit(solution)/shard_map/psum | solution.py:115
  391.1 56.3 %copy-start.1 = (bf16[768,1536]{1,0:T(8,128)(2,1)S(1)}, bf16[768,1536]{1,0:T(8,128)(2,1)}, u32[]{:S(2)}) copy-start(bf16[768,1536]{1,0:T(8,128)(2,1)} %param.13) | copy-start | bytes 7077892
Sparse Core Ops, SparseCore 0:
  402.4 43.2 all-reduce.1
where the time goes:
time: 457 us; the launch traced here: 454 us
  waiting for transfers between devices  287 us (63%)
  local copies, waits for them, and re-layouts  62.5 us (14%)
  matrix products  37.5 us (8%)
  blocking collectives  22.2 us (5%)
  other arithmetic  17 us (4%)
  starting transfers between devices  14.4 us (3%)
  between operations  13.6 us (3%)
    all_to_all x1, waiting for transfers between devices, body(): lax.all_to_all(reply_rows, 'img', split_axis=0, concat_axis=0, tiled=True)  139 us
    all_to_all x1, waiting for transfers between devices, body(): lax.all_to_all(outgoing, 'img', split_axis=0, concat_axis=0, tiled=True)  105 us
    psum x1, waiting for transfers between devices, body(): image_sums = lax.psum(partial_sums.astype(jnp.bfloat16), 'rep')  43.4 us
    all_to_all x1, blocking collectives, body(): lax.all_to_all(request, 'img', split_axis=0, concat_axis=0, tiled=True)  22.2 us
    dot_general x1, matrix products, body(): jnp.dot(expanded.astype(jnp.bfloat16), mlp_down, preferred_element_type=j...  16.6 us
    sub x1, other arithmetic, attend(): scores = scores - jnp.max(scores, axis=-1, keepdims=True)  12.9 us
  transfers between devices with their start and end apart: 3, of which 3 were waited for; matrix products, arithmetic and copies ran while one was open for 0% of the time, Pallas kernels for 0%

commit v1 on v0

v1 whole, which is shorter than its diff:
```python
import jax
import jax.numpy as jnp
from jax import lax
from jax.experimental import pallas as pl
from jax.experimental.pallas import tpu as pltpu
from jax.sharding import PartitionSpec as P

HEAD_DIM = 64
TOK = 24
IMG_DEV = 8
NX, NY, NZ = 4, 4, 8
BLK = IMG_DEV * TOK
SIDE = 4 * BLK
DEVS = NX * NY * NZ * 2
PAIR_DEV = 32
GROUP = 8
SLOTS = 64
MESH = pl.DeviceIdType.MESH
F32 = jnp.float32
BF16 = jnp.bfloat16


def place():
    img = lax.axis_index("img")
    return img // 8, (img // 2) % 4, img % 2, lax.axis_index("rep")


def dev(z, x, c, y):
    return ((z * NX + x) * 2 + c, y)


def remote(src, dst, send, recv, to):
    return pltpu.make_async_remote_copy(
        src_ref=src,
        dst_ref=dst,
        send_sem=send,
        recv_sem=recv,
        device_id=to,
        device_id_type=MESH,
    )


def peers_of(z, x, c, y):
    peers = []
    for d in range(1, 8):
        k = (x * 2 + c + d) % 8
        peers.append(dev(z, k // 2, k % 2, y))
    for d in range(1, NZ):
        peers.append(dev((z + d) % NZ, x, c, y))
    for d in range(1, NY):
        peers.append(dev(z, x, c, (y + d) % NY))
    return peers


def barrier_all(z, x, c, y):
    barrier = pltpu.get_barrier_semaphore()
    peers = peers_of(z, x, c, y)
    for p in peers:
        pl.semaphore_signal(barrier, inc=1, device_id=p, device_id_type=MESH)
    return barrier, len(peers)


def gather_kernel(
    tok_ref,
    proj_ref,
    mine_ref,
    a_out,
    b_out,
    list_out,
    own,
    a_send,
    a_recv,
    b_send,
    b_recv,
    f_send,
    f_recv,
    loc,
    lx_send,
    lx_recv,
    lz_send,
    lz_recv,
    ly_send,
    ly_recv,
):
    z, x, c, y = place()
    barrier, n_peers = barrier_all(z, x, c, y)
    me8 = x * 2 + c
    row0 = y * 64 + z * 8
    list_out[pl.ds(row0 + me8, 1)] = mine_ref[...]
    own[...] = jnp.dot(tok_ref[...], proj_ref[...], preferred_element_type=F32).astype(BF16)
    pl.semaphore_wait(barrier, n_peers)

    lx = []
    for d in range(1, 8):
        k = (me8 + d) % 8
        mine = list_out.at[pl.ds(row0 + me8, 1)]
        cp = remote(mine, mine, lx_send.at[d], lx_recv.at[d], dev(z, k // 2, k % 2, y))
        cp.start()
        lx.append(cp)

    s_b = (z // 4) * 2 + c
    b_dst = b_out.at[pl.ds(pl.multiple_of(s_b * BLK, BLK), BLK)]
    z0 = (z - y + NZ) % NZ
    z1 = (z - y + NZ + 4) % NZ
    self_b = y == 0
    b1 = remote(own, b_dst, b_send.at[1], b_recv.at[z // 4], dev(z1, x, c, y))
    b1.start()
    b0 = remote(own, b_dst, b_send.at[0], b_recv.at[z // 4], dev(z0, x, c, y))
    b0_local = pltpu.make_async_copy(own, b_dst, loc.at[0])

    @pl.when(jnp.logical_not(self_b))
    def _():
        b0.start()

    @pl.when(self_b)
    def _():
        b0_local.start()

    s_a = (x % 2) * 2 + c
    a_dst = a_out.at[pl.ds(pl.multiple_of(s_a * BLK, BLK), BLK)]
    half = x // 2
    self_a = half == c
    a_cps = []
    for d in (2, 1, 3):
        cp = remote(own, a_dst, a_send.at[d], a_recv.at[s_a], dev(z, (x + d) % NX, half, y))
        cp.start()
        a_cps.append(cp)
    a0 = remote(own, a_dst, a_send.at[0], a_recv.at[s_a], dev(z, x, half, y))
    a0_local = pltpu.make_async_copy(own, a_dst, loc.at[1])

    @pl.when(jnp.logical_not(self_a))
    def _():
        a0.start()

    @pl.when(self_a)
    def _():
        a0_local.start()

    for cp in lx:
        cp.wait_recv()
    lz = []
    for d in range(1, NZ):
        rows = list_out.at[pl.ds(row0, 8)]
        cp = remote(rows, rows, lz_send.at[d], lz_recv.at[d], dev((z + d) % NZ, x, c, y))
        cp.start()
        lz.append(cp)
    for cp in lz:
        cp.wait_recv()
    ly = []
    for d in range(1, NY):
        rows = list_out.at[pl.ds(y * 64, 64)]
        cp = remote(rows, rows, ly_send.at[d], ly_recv.at[d], dev(z, x, c, (y + d) % NY))
        cp.start()
        ly.append(cp)

    sib = dev(z, x, 1 - c, y)
    fwd = []
    for t in range(2):
        slot = b_out.at[pl.ds(pl.multiple_of((t * 2 + c) * BLK, BLK), BLK)]
        arrived = remote(own, slot, b_send.at[t], b_recv.at[t], sib)
        here = jnp.logical_and(self_b, z // 4 == t)

        @pl.when(jnp.logical_not(here))
        def _(arrived=arrived):
            arrived.wait_recv()

        @pl.when(here)
        def _():
            b0_local.wait()

        cp = remote(slot, slot, f_send.at[t], f_recv.at[t], sib)
        cp.start()
        fwd.append(cp)

    for s in range(4):
        slot = a_out.at[pl.ds(s * BLK, BLK)]
        arrived = remote(own, slot, a_send.at[0], a_recv.at[s], sib)
        here = jnp.logical_and(self_a, s_a == s)

        @pl.when(jnp.logical_not(here))
        def _(arrived=arrived):
            arrived.wait_recv()

        @pl.when(here)
        def _():
            a0_local.wait()

    for t in range(2):
        slot = b_out.at[pl.ds(pl.multiple_of((t * 2 + 1 - c) * BLK, BLK), BLK)]
        remote(slot, slot, f_send.at[t], f_recv.at[t], sib).wait_recv()
    for cp in ly:
        cp.wait_recv()

    for cp in lx + lz + ly + a_cps + fwd + [b1]:
        cp.wait_send()

    @pl.when(jnp.logical_not(self_b))
    def _():
        b0.wait_send()

    @pl.when(jnp.logical_not(self_a))
    def _():
        a0.wait_send()


def gather(tokens, proj_in, mine):
    width = proj_in.shape[1]
    dma = pltpu.SemaphoreType.DMA
    vmem = pl.BlockSpec(memory_space=pltpu.VMEM)
    anym = pl.BlockSpec(memory_space=pl.ANY)
    return pl.pallas_call(
        gather_kernel,
        out_shape=(
            jax.ShapeDtypeStruct((SIDE, width), BF16),
            jax.ShapeDtypeStruct((SIDE, width), BF16),
            jax.ShapeDtypeStruct((DEVS, 1, 128), jnp.int32),
        ),
        in_specs=[vmem] * 3,
        out_specs=(anym, anym, vmem),
        scratch_shapes=[
            pltpu.VMEM((BLK, width), BF16),
            dma((4,)),
            dma((4,)),
            dma((2,)),
            dma((2,)),
            dma((2,)),
            dma((2,)),
            dma((2,)),
            dma((8,)),
            dma((8,)),
            dma((8,)),
            dma((8,)),
            dma((4,)),
            dma((4,)),
        ],
        compiler_params=pltpu.CompilerParams(
            collective_id=0, has_side_effects=True, vmem_limit_bytes=32 * 1024 * 1024
        ),
        name="gather_blocks",
    )(tokens, proj_in, mine)


def norm(v):
    centred = v - jnp.mean(v, axis=-1, keepdims=True)
    spread = jnp.mean(centred * centred, axis=-1, keepdims=True)
    return centred * lax.rsqrt(spread + 1e-06)


def cell_kernel(
    ids_ref,
    table_ref,
    list_ref,
    a_ref,
    b_ref,
    wq_hbm,
    wkv_hbm,
    wo_hbm,
    up_hbm,
    down_hbm,
    pa_ref,
    pb_ref,
    wq,
    wkv,
    wo,
    up,
    down,
    side,
    qs,
    ks,
    vs,
    acc_a,
    acc_b,
    rank_t,
    val_t,
    slots_v,
    slots_s,
    att,
    ffn,
    sems,
):
    width = wq.shape[0]
    heads_quad = 4
    quad = heads_quad * HEAD_DIM
    copies = [
        pltpu.make_async_copy(h, v, sems.at[i])
        for i, (h, v) in enumerate(
            ((wq_hbm, wq), (wkv_hbm, wkv), (wo_hbm, wo), (up_hbm, up), (down_hbm, down))
        )
    ]
    for cp in copies:
        cp.start()

    a_id, b_x, b_j = ids_ref[0], ids_ref[1], ids_ref[2]
    flat = list_ref[...].reshape(DEVS, 128)
    flat_t = flat.astype(F32).T.astype(jnp.int32)
    a_img = flat_t[:PAIR_DEV]
    b_img = flat_t[PAIR_DEV : 2 * PAIR_DEV]
    level = flat_t[2 * PAIR_DEV : 3 * PAIR_DEV]
    hit = (
        (lax.shift_right_logical(a_img, 5) == a_id)
        & ((lax.shift_right_logical(b_img, 4) & 3) == b_x)
        & ((lax.shift_right_logical(b_img, 6) & 3) == b_j)
    )
    hit_f = hit.astype(F32)
    r_i = lax.broadcasted_iota(jnp.int32, (DEVS, DEVS), 0)
    c_i = lax.broadcasted_iota(jnp.int32, (DEVS, DEVS), 1)
    upper = (r_i <= c_i).astype(BF16)
    across = jnp.dot(hit_f.astype(BF16), upper, preferred_element_type=F32)
    totals = across[:, DEVS - 1 : DEVS]
    k_r = lax.broadcasted_iota(jnp.int32, (PAIR_DEV, PAIR_DEV), 0)
    k_c = lax.broadcasted_iota(jnp.int32, (PAIR_DEV, PAIR_DEV), 1)
    lower = (k_c < k_r).astype(BF16)
    before = jnp.dot(
        lower,
        jnp.broadcast_to(totals, (PAIR_DEV, 128)).astype(BF16),
        preferred_element_type=F32,
    )[:, :1]
    rank = (across + before).astype(jnp.int32) - 1
    rank_t[...] = jnp.where(hit, rank, -1)
    val_t[...] = ((a_img & 31) * 32 + (lax.shift_right_logical(b_img, 8) * 16 + (b_img & 15))) * 16 + level
    count = jnp.sum(hit_f).astype(jnp.int32)

    acc_a[...] = jnp.zeros_like(acc_a)
    acc_b[...] = jnp.zeros_like(acc_b)

    copies[0].wait()
    copies[1].wait()
    for i in range(4):
        rows = pl.ds(i * BLK, BLK)
        q_side = a_ref[rows, :].astype(F32)
        side[pl.ds(i * IMG_DEV, IMG_DEV)] = q_side.reshape(IMG_DEV, TOK, width)
        qn = norm(q_side).astype(BF16)
        q = jnp.dot(qn, wq[...], preferred_element_type=F32).astype(BF16).astype(F32)
        qs[pl.ds(i * IMG_DEV, IMG_DEV)] = (q * (HEAD_DIM**-0.5)).reshape(IMG_DEV, TOK, width)
        mn = norm(b_ref[rows, :].astype(F32)).astype(BF16)
        k = jnp.dot(mn, wkv[:, :width], preferred_element_type=F32)
        ks[pl.ds(i * IMG_DEV, IMG_DEV)] = k.reshape(IMG_DEV, TOK, width)
        v = jnp.dot(mn, wkv[:, width:], preferred_element_type=F32)
        vs[pl.ds(i * IMG_DEV, IMG_DEV)] = v.reshape(IMG_DEV, TOK, width)
    for cp in copies[2:]:
        cp.wait()

    lane_head = lax.broadcasted_iota(jnp.int32, (TOK, quad), 1) // HEAD_DIM

    def attend(a_loc, b_loc):
        out = []
        for p in range(width // quad):
            cols = slice(p * quad, (p + 1) * quad)
            q = qs[a_loc, :, cols]
            k = ks[b_loc, :, cols].astype(BF16)
            v = vs[b_loc, :, cols].astype(BF16)
            q4 = jnp.concatenate(
                [jnp.where(lane_head == h, q, 0.0) for h in range(heads_quad)], axis=0
            ).astype(BF16)
            s = lax.dot_general(q4, k, (((1,), (1,)), ((), ())), preferred_element_type=F32)
            e = jnp.exp(s - jnp.max(s, axis=-1, keepdims=True))
            probs = (e / jnp.sum(e, axis=-1, keepdims=True)).astype(BF16)
            r = jnp.dot(probs, v, preferred_element_type=F32)
            o = r[3 * TOK :]
            for h in (2, 1, 0):
                o = jnp.where(lane_head == h, r[h * TOK : (h + 1) * TOK], o)
            out.append(o)
        return jnp.concatenate(out, axis=1)

    def slot_block(block, carry):
        base = block * SLOTS
        slot = lax.broadcasted_iota(jnp.int32, (SLOTS, DEVS), 0) + base
        found = jnp.zeros((SLOTS, DEVS), jnp.int32)
        for k in range(PAIR_DEV):
            found += jnp.where(rank_t[k : k + 1, :] == slot, val_t[k : k + 1, :], 0)
        col = jnp.sum(found.astype(F32), axis=1, keepdims=True).astype(jnp.int32)
        slots_v[...] = jnp.broadcast_to(col, (SLOTS, 128))
        cp = pltpu.make_async_copy(slots_v, slots_s, sems.at[5])
        cp.start()
        cp.wait()
        here = jnp.minimum(count - base, SLOTS)

        def group(g, carry2):
            locs = []
            for i in range(GROUP):
                word = slots_s[g * GROUP + i, 0]
                a_loc = word // 512
                b_loc = (word // 16) % 32
                locs.append((a_loc, b_loc, word % 16))
                att[pl.ds(i * TOK, TOK), :] = attend(a_loc, b_loc)
            query = jnp.concatenate([side[a_loc] for a_loc, _, _ in locs], axis=0)
            hidden = query + jnp.dot(
                att[...].astype(BF16), wo[...], preferred_element_type=F32
            )
            hn = norm(hidden).astype(BF16)
            u = jnp.dot(hn, up[...], preferred_element_type=F32)
            ex = (0.5 * u) * (1.0 + lax.erf(u * (0.5**0.5)))
            out = hidden + jnp.dot(ex.astype(BF16), down[...], preferred_element_type=F32)
            ffn[...] = out
            for i in range(GROUP):
                a_loc, b_loc, lev = locs[i]

                @pl.when(g * GROUP + i < here)
                def _(i=i, a_loc=a_loc, b_loc=b_loc, lev=lev):
                    feature = table_ref[lev] * ffn[pl.ds(i * TOK, TOK), :]
                    feature = feature.astype(BF16).astype(F32)
                    acc_a[a_loc] = acc_a[a_loc] + feature
                    acc_b[b_loc] = acc_b[b_loc] + feature

            return carry2

        lax.fori_loop(0, (here + GROUP - 1) // GROUP, group, 0)
        return carry

    lax.fori_loop(0, (count + SLOTS - 1) // SLOTS, slot_block, 0)
    pa_ref[...] = acc_a[...].reshape(SIDE, width).astype(BF16)
    pb_ref[...] = acc_b[...].reshape(SIDE, width).astype(BF16)


def cell(ids, table, pairs, a_blk, b_blk, wq, wkv, wo, up, down, interpret=False):
    width, ff = up.shape
    vmem = pl.BlockSpec(memory_space=pltpu.VMEM)
    smem = pl.BlockSpec(memory_space=pltpu.SMEM)
    anym = pl.BlockSpec(memory_space=pl.ANY)
    images = 4 * IMG_DEV
    return pl.pallas_call(
        cell_kernel,
        out_shape=(
            jax.ShapeDtypeStruct((SIDE, width), BF16),
            jax.ShapeDtypeStruct((SIDE, width), BF16),
        ),
        in_specs=[smem, smem, vmem, vmem, vmem] + [anym] * 5,
        out_specs=(vmem, vmem),
        scratch_shapes=[
            pltpu.VMEM((width, width), BF16),
            pltpu.VMEM((width, 2 * width), BF16),
            pltpu.VMEM((width, width), BF16),
            pltpu.VMEM((width, ff), BF16),
            pltpu.VMEM((ff, width), BF16),
            pltpu.VMEM((images, TOK, width), F32),
            pltpu.VMEM((images, TOK, width), F32),
            pltpu.VMEM((images, TOK, width), F32),
            pltpu.VMEM((images, TOK, width), F32),
            pltpu.VMEM((images, TOK, width), F32),
            pltpu.VMEM((images, TOK, width), F32),
            pltpu.VMEM((PAIR_DEV, DEVS), jnp.int32),
            pltpu.VMEM((PAIR_DEV, DEVS), jnp.int32),
            pltpu.VMEM((SLOTS, 128), jnp.int32),
            pltpu.SMEM((SLOTS, 128), jnp.int32),
            pltpu.VMEM((GROUP * TOK, width), F32),
            pltpu.VMEM((GROUP * TOK, width), F32),
            pltpu.SemaphoreType.DMA((6,)),
        ],
        compiler_params=pltpu.CompilerParams(vmem_limit_bytes=52 * 1024 * 1024),
        name="cell_pairs",
        interpret=interpret,
    )(ids, table, pairs, a_blk, b_blk, wq, wkv, wo, up, down)


def reduce_kernel(
    pa_ref,
    pb_ref,
    out_ref,
    ra,
    rsib,
    sb,
    rz,
    tot,
    ry,
    a_send,
    a_recv,
    s_send,
    s_recv,
    z_send,
    z_recv,
    y_send,
    y_recv,
    o_send,
    o_recv,
):
    z, x, c, y = place()
    barrier, n_peers = barrier_all(z, x, c, y)
    pl.semaphore_wait(barrier, n_peers)
    sib = dev(z, x, 1 - c, y)

    def rows(s):
        return pl.ds(pl.multiple_of(s * BLK, BLK), BLK)

    sib_cps = []
    for t in range(2):
        cp = remote(pb_ref.at[rows(t * 2 + 1 - c)], rsib.at[t], s_send.at[t], s_recv.at[t], sib)
        cp.start()
        sib_cps.append(cp)

    a_cps = []
    for s in range(4):
        xt = 2 * c + s // 2
        here = jnp.logical_and(xt == x, c == s % 2)
        cp = remote(pa_ref.at[rows(s)], ra.at[x], a_send.at[s], a_recv.at[x], dev(z, xt, s % 2, y))
        a_cps.append((here, cp))

        @pl.when(jnp.logical_not(here))
        def _(cp=cp):
            cp.start()

        @pl.when(here)
        def _(s=s):
            ra[x] = pa_ref[rows(s), :]

    j = (z + y) % 4
    z_cps = []
    for t in range(2):
        sib_cps[t].wait_recv()
        total = pb_ref[rows(t * 2 + c), :].astype(F32) + rsib[t].astype(F32)
        sb[t] = total.astype(BF16)
        zt = j + 4 * t
        here = zt == z
        cp = remote(sb.at[t], rz.at[z // 4], z_send.at[t], z_recv.at[z // 4], dev(zt, x, c, y))
        z_cps.append((here, cp))

        @pl.when(jnp.logical_not(here))
        def _(cp=cp):
            cp.start()

        @pl.when(here)
        def _(t=t):
            rz[t] = sb[t]

    for s in range(4):
        here = jnp.logical_and(s == x, x // 2 == c)

        @pl.when(jnp.logical_not(here))
        def _(s=s):
            remote(pa_ref.at[rows(0)], ra.at[s], a_send.at[0], a_recv.at[s], sib).wait_recv()

    total = ra[0].astype(F32) + ra[1].astype(F32) + ra[2].astype(F32) + ra[3].astype(F32)
    for t in range(2):
        here = jnp.logical_and(y == 0, z // 4 == t)

        @pl.when(jnp.logical_not(here))
        def _(t=t):
            remote(sb.at[t], rz.at[t], z_send.at[0], z_recv.at[t], sib).wait_recv()

    tot[...] = (total + rz[0].astype(F32) + rz[1].astype(F32)).astype(BF16)

    part = BLK // NY

    def y_rows(yy):
        return pl.ds(pl.multiple_of(yy * part, part), part)

    y_cps = []
    for d in range(1, NY):
        yt = (y + d) % NY
        cp = remote(tot.at[y_rows(yt)], ry.at[d], y_send.at[d], y_recv.at[d], dev(z, x, c, yt))
        cp.start()
        y_cps.append(cp)
    mine = tot[y_rows(y), :].astype(F32)
    for d in range(1, NY):
        y_cps[d - 1].wait_recv()
        mine = mine + ry[d].astype(F32)
    out_ref[y_rows(y), :] = mine.astype(BF16)
    o_cps = []
    for d in range(1, NY):
        yt = (y + d) % NY
        piece = out_ref.at[y_rows(y)]
        cp = remote(piece, piece, o_send.at[d], o_recv.at[d], dev(z, x, c, yt))
        cp.start()
        o_cps.append(cp)
    for d in range(1, NY):
        piece = out_ref.at[y_rows((y - d + NY) % NY)]
        remote(piece, piece, o_send.at[d], o_recv.at[d], sib).wait_recv()

    for cp in sib_cps + y_cps + o_cps:
        cp.wait_send()
    for here, cp in a_cps + z_cps:

        @pl.when(jnp.logical_not(here))
        def _(cp=cp):
            cp.wait_send()


def reduce_back(pa, pb):
    width = pa.shape[1]
    dma = pltpu.SemaphoreType.DMA
    vmem = pl.BlockSpec(memory_space=pltpu.VMEM)
    return pl.pallas_call(
        reduce_kernel,
        out_shape=jax.ShapeDtypeStruct((BLK, width), BF16),
        in_specs=[vmem] * 2,
        out_specs=vmem,
        scratch_shapes=[
            pltpu.VMEM((4, BLK, width), BF16),
            pltpu.VMEM((2, BLK, width), BF16),
            pltpu.VMEM((2, BLK, width), BF16),
            pltpu.VMEM((2, BLK, width), BF16),
            pltpu.VMEM((BLK, width), BF16),
            pltpu.VMEM((NY, BLK // NY, width), BF16),
            dma((4,)),
            dma((4,)),
            dma((2,)),
            dma((2,)),
            dma((2,)),
            dma((2,)),
            dma((4,)),
            dma((4,)),
            dma((4,)),
            dma((4,)),
        ],
        compiler_params=pltpu.CompilerParams(
            collective_id=1, has_side_effects=True, vmem_limit_bytes=32 * 1024 * 1024
        ),
        name="reduce_back",
    )(pa, pb)


def body(
    tokens,
    proj_in,
    attn_query,
    attn_keyval,
    attn_output,
    mlp_up,
    mlp_down,
    pair_list,
    conf_level,
    conf_table,
):
    img_dev, tok_count, enc_width = tokens.shape
    z, x, c, y = place()
    mine = jnp.concatenate(
        [pair_list[:, 0], pair_list[:, 1], conf_level, jnp.zeros((PAIR_DEV,), jnp.int32)]
    ).reshape(1, 1, 128)
    a_blk, b_blk, pairs = gather(tokens.reshape(img_dev * tok_count, enc_width), proj_in, mine)
    ids = jnp.stack([z * 2 + c, x, (z + y) % 4, 0]).astype(jnp.int32)
    pa, pb = cell(
        ids, conf_table, pairs, a_blk, b_blk, attn_query, attn_keyval, attn_output, mlp_up, mlp_down
    )
    joined = reduce_back(pa, pb)
    return joined.reshape(img_dev, tok_count, joined.shape[1])


def solution(mesh):
    placed = (
        P("img", None, None),
        P(),
        P(),
        P(),
        P(),
        P(),
        P(),
        P(("img", "rep"), None),
        P(("img", "rep")),
        P(),
    )
    return jax.shard_map(
        body, mesh=mesh, in_specs=placed, out_specs=P("img", None, None), check_vma=False
    )
```

time: 457 us -> 111 us (0.24)
  the two profiles are of different devices: /device:TPU:1 before, /device:TPU:2 now
where the time goes in v1:
time: 111 us; the launch traced here: 110 us
  Pallas kernels  102 us (92%)
  local copies, waits for them, and re-layouts  7.22 us (7%)
    pallas_call x1, Pallas kernels, reduce_back(): pl.pallas_call(reduce_kernel, out_shape=jax.ShapeDtypeStruct((BLK, width)...  40.2 us
    pallas_call x1, Pallas kernels, gather(): pl.pallas_call(gather_kernel, out_shape=(jax.ShapeDtypeStruct((SIDE, widt...  34.2 us
    pallas_call x1, Pallas kernels, cell(): pl.pallas_call(cell_kernel, out_shape=(jax.ShapeDtypeStruct((SIDE, width)...  27.8 us
    unnamed x13, local copies, waits for them, and re-layouts  6.46 us

profile of v1, /device:TPU:2, one launch (start us, length us, event | category | flops | bytes accessed | tf_op | source)
XLA Modules:
  0.0 110.3 jit_solution(8962593981040297305)
XLA Ops:
  0.0 0.0 copy-start.5
  0.0 0.1 pad_add_fusion.ids_ref
  0.1 0.8 slice_bitcast_fusion.1
  0.8 0.7 add_bitcast_fusion.mine_ref
  1.6 0.0 copy-start
  1.6 1.4 %copy-done = bf16[1024,768]{1,0:T(8,128)(2,1)S(1)} copy-done((bf16[1024,768]{1,0:T(8,128)(2,1)S(1)}, bf16[1024,768]{1,0:T(8,128)(2,1)}, u32[]{:S(2)}) %copy-start) | copy-done | bytes 1572888
  3.0 0.0 copy-start.4
  3.0 1.0 copy-done.4
  4.0 34.2 %gather_blocks.1 = (bf16[768,768]{1,0:T(8,128)(2,1)S(1)}, bf16[768,768]{1,0:T(8,128)(2,1)S(1)}, s32[256,1,128]{2,1,0:T(1,128)S(1)}) custom-call(bf16[192,1024]{1,0:T(8,128)(2,1)S(1)} %bitcast.12, bf16[1024,768]{1,0:T(8,128)(2,1)S(1)} %copy-done, s32[1,1,128]{2,1,0:T(1,128)S(1)} %add_bitcast_fusion.mine_ref), custom_call_target="tpu_custom_call" | custom-call | tf_op jit(solution)/shard_map/gather_blocks/pallas_call | solution.py:211
  38.2 0.0 copy-start.1
  38.2 1.0 copy-done.1
  39.2 0.0 copy-start.2
  39.2 1.0 copy-done.2
  40.2 0.0 copy-done.5
  40.3 27.8 %cell_pairs.1 = (bf16[768,768]{1,0:T(8,128)(2,1)S(1)}, bf16[768,768]{1,0:T(8,128)(2,1)}) custom-call(s32[4]{0:T(128)S(1)} %pad_add_fusion.ids_ref, f32[16]{0:T(128)S(1)} %copy-done.5, s32[256,1,128]{2,1,0:T(1,128)S(1)} %get-tuple-element.10.list_ref, bf16[768,768]{1,0:T(8,128)(2,1)} %copy-done.1, bf16[768,768]{1,0:T(8,128)(2,1)} %copy-done.2, ...), custom_call_target="tpu_custom_call" | custom-call | tf_op jit(solution)/shard_map/cell_pairs/pallas_call | solution.py:421
  68.1 0.0 copy-start.3
  68.1 1.3 %copy-done.3 = bf16[768,768]{1,0:T(8,128)(2,1)S(1)} copy-done((bf16[768,768]{1,0:T(8,128)(2,1)S(1)}, bf16[768,768]{1,0:T(8,128)(2,1)}, u32[]{:S(2)}) %copy-start.3) | copy-done | bytes 1179672
  69.4 40.2 %reduce_back.1 = bf16[192,768]{1,0:T(8,128)(2,1)S(1)} custom-call(bf16[768,768]{1,0:T(8,128)(2,1)S(1)} %get-tuple-element.13.pa_ref, bf16[768,768]{1,0:T(8,128)(2,1)S(1)} %copy-done.3), custom_call_target="tpu_custom_call" | custom-call | tf_op jit(solution)/shard_map/reduce_back/pallas_call | solution.py:581
  109.6 0.7 copy.12
  (1 shorter events, 0.0 us)
Async XLA Ops:
  0.0 40.2 %copy-start.5 = (f32[16]{0:T(128)S(1)}, f32[16]{0:T(128)}, u32[]{:S(2)}) copy-start(f32[16]{0:T(128)} %table_ref.1) | copy-start | bytes 196
  1.6 1.4 %copy-start = (bf16[1024,768]{1,0:T(8,128)(2,1)S(1)}, bf16[1024,768]{1,0:T(8,128)(2,1)}, u32[]{:S(2)}) copy-start(bf16[1024,768]{1,0:T(8,128)(2,1)} %proj_ref.1) | copy-start | bytes 4718596
  3.0 1.0 copy-start.4
  38.2 1.0 copy-start.1
  39.2 1.0 copy-start.2
  68.1 1.3 %copy-start.3 = (bf16[768,768]{1,0:T(8,128)(2,1)S(1)}, bf16[768,768]{1,0:T(8,128)(2,1)}, u32[]{:S(2)}) copy-start(bf16[768,768]{1,0:T(8,128)(2,1)} %get-tuple-element.14.pb_ref) | copy-start | bytes 3538948

commit v2 on v1

--- a/solution.py
+++ b/solution.py
@@ -15,6 +15,8 @@
 PAIR_DEV = 32
 GROUP = 8
 SLOTS = 64
+CHUNKS = 2
+CHUNK = BLK // CHUNKS
 MESH = pl.DeviceIdType.MESH
 F32 = jnp.float32
 BF16 = jnp.bfloat16
@@ -61,12 +63,15 @@
 
 
 def gather_kernel(
-    tok_ref,
-    proj_ref,
-    mine_ref,
+    tok_hbm,
+    proj_hbm,
+    pair_ref,
+    level_ref,
     a_out,
     b_out,
     list_out,
+    tok,
+    proj,
     own,
     a_send,
     a_recv,
@@ -83,20 +88,28 @@
     ly_recv,
 ):
     z, x, c, y = place()
+    tok_in = pltpu.make_async_copy(tok_hbm, tok, loc.at[2])
+    proj_in = pltpu.make_async_copy(proj_hbm, proj, loc.at[3])
+    tok_in.start()
+    proj_in.start()
     barrier, n_peers = barrier_all(z, x, c, y)
     me8 = x * 2 + c
-    row0 = y * 64 + z * 8
-    list_out[pl.ds(row0 + me8, 1)] = mine_ref[...]
-    own[...] = jnp.dot(tok_ref[...], proj_ref[...], preferred_element_type=F32).astype(BF16)
+    row_me = y * 64 + me8 * 8 + z
+    list_out[row_me, :, 0:PAIR_DEV] = pair_ref[0:1, :]
+    list_out[row_me, :, PAIR_DEV : 2 * PAIR_DEV] = pair_ref[1:2, :]
+    list_out[row_me, :, 2 * PAIR_DEV : 3 * PAIR_DEV] = level_ref[...]
+    list_out[row_me, :, 3 * PAIR_DEV :] = jnp.zeros((1, 128 - 3 * PAIR_DEV), jnp.int32)
     pl.semaphore_wait(barrier, n_peers)
 
-    lx = []
-    for d in range(1, 8):
-        k = (me8 + d) % 8
-        mine = list_out.at[pl.ds(row0 + me8, 1)]
-        cp = remote(mine, mine, lx_send.at[d], lx_recv.at[d], dev(z, k // 2, k % 2, y))
-        cp.start()
-        lx.append(cp)
+    lz = []
+    for d in range(1, NZ):
+        mine = list_out.at[pl.ds(row_me, 1)]
+        cp = remote(mine, mine, lz_send.at[d], lz_recv.at[d], dev((z + d) % NZ, x, c, y))
+        cp.start()
+        lz.append(cp)
+    tok_in.wait()
+    proj_in.wait()
+    own[...] = jnp.dot(tok[...], proj[...], preferred_element_type=F32).astype(BF16)
 
     s_b = (z // 4) * 2 + c
     b_dst = b_out.at[pl.ds(pl.multiple_of(s_b * BLK, BLK), BLK)]
@@ -116,6 +129,16 @@
     def _():
         b0_local.start()
 
+    for cp in lz:
+        cp.wait_recv()
+    lx = []
+    for d in range(1, 8):
+        k = (me8 + d) % 8
+        rows = list_out.at[pl.ds(y * 64 + me8 * 8, 8)]
+        cp = remote(rows, rows, lx_send.at[d], lx_recv.at[d], dev(z, k // 2, k % 2, y))
+        cp.start()
+        lx.append(cp)
+
     s_a = (x % 2) * 2 + c
     a_dst = a_out.at[pl.ds(pl.multiple_of(s_a * BLK, BLK), BLK)]
     half = x // 2
@@ -138,14 +161,6 @@
 
     for cp in lx:
         cp.wait_recv()
-    lz = []
-    for d in range(1, NZ):
-        rows = list_out.at[pl.ds(row0, 8)]
-        cp = remote(rows, rows, lz_send.at[d], lz_recv.at[d], dev((z + d) % NZ, x, c, y))
-        cp.start()
-        lz.append(cp)
-    for cp in lz:
-        cp.wait_recv()
     ly = []
     for d in range(1, NY):
         rows = list_out.at[pl.ds(y * 64, 64)]
@@ -203,7 +218,7 @@
         a0.wait_send()
 
 
-def gather(tokens, proj_in, mine):
+def gather(tokens, proj_in, pairs_t, levels):
     width = proj_in.shape[1]
     dma = pltpu.SemaphoreType.DMA
     vmem = pl.BlockSpec(memory_space=pltpu.VMEM)
@@ -215,9 +230,11 @@
             jax.ShapeDtypeStruct((SIDE, width), BF16),
             jax.ShapeDtypeStruct((DEVS, 1, 128), jnp.int32),
         ),
-        in_specs=[vmem] * 3,
+        in_specs=[anym, anym, vmem, vmem],
         out_specs=(anym, anym, vmem),
         scratch_shapes=[
+            pltpu.VMEM(tokens.shape, BF16),
+            pltpu.VMEM(proj_in.shape, BF16),
             pltpu.VMEM((BLK, width), BF16),
             dma((4,)),
             dma((4,)),
@@ -225,7 +242,7 @@
             dma((2,)),
             dma((2,)),
             dma((2,)),
-            dma((2,)),
+            dma((4,)),
             dma((8,)),
             dma((8,)),
             dma((8,)),
@@ -237,7 +254,7 @@
             collective_id=0, has_side_effects=True, vmem_limit_bytes=32 * 1024 * 1024
         ),
         name="gather_blocks",
-    )(tokens, proj_in, mine)
+    )(tokens, proj_in, pairs_t, levels)
 
 
 def norm(v):
@@ -250,8 +267,8 @@
     ids_ref,
     table_ref,
     list_ref,
-    a_ref,
-    b_ref,
+    a_hbm,
+    b_hbm,
     wq_hbm,
     wkv_hbm,
     wo_hbm,
@@ -259,6 +276,8 @@
     down_hbm,
     pa_ref,
     pb_ref,
+    a_ref,
+    b_ref,
     wq,
     wkv,
     wo,
@@ -284,7 +303,15 @@
     copies = [
         pltpu.make_async_copy(h, v, sems.at[i])
         for i, (h, v) in enumerate(
-            ((wq_hbm, wq), (wkv_hbm, wkv), (wo_hbm, wo), (up_hbm, up), (down_hbm, down))
+            (
+                (a_hbm, a_ref),
+                (wq_hbm, wq),
+                (b_hbm, b_ref),
+                (wkv_hbm, wkv),
+                (wo_hbm, wo),
+                (up_hbm, up),
+                (down_hbm, down),
+            )
         )
     ]
     for cp in copies:
@@ -323,8 +350,8 @@
     acc_a[...] = jnp.zeros_like(acc_a)
     acc_b[...] = jnp.zeros_like(acc_b)
 
-    copies[0].wait()
-    copies[1].wait()
+    for cp in copies[:4]:
+        cp.wait()
     for i in range(4):
         rows = pl.ds(i * BLK, BLK)
         q_side = a_ref[rows, :].astype(F32)
@@ -337,7 +364,7 @@
         ks[pl.ds(i * IMG_DEV, IMG_DEV)] = k.reshape(IMG_DEV, TOK, width)
         v = jnp.dot(mn, wkv[:, width:], preferred_element_type=F32)
         vs[pl.ds(i * IMG_DEV, IMG_DEV)] = v.reshape(IMG_DEV, TOK, width)
-    for cp in copies[2:]:
+    for cp in copies[4:]:
         cp.wait()
 
     lane_head = lax.broadcasted_iota(jnp.int32, (TOK, quad), 1) // HEAD_DIM
@@ -352,10 +379,10 @@
             q4 = jnp.concatenate(
                 [jnp.where(lane_head == h, q, 0.0) for h in range(heads_quad)], axis=0
             ).astype(BF16)
-            s = lax.dot_general(q4, k, (((1,), (1,)), ((), ())), preferred_element_type=F32)
-            e = jnp.exp(s - jnp.max(s, axis=-1, keepdims=True))
-            probs = (e / jnp.sum(e, axis=-1, keepdims=True)).astype(BF16)
-            r = jnp.dot(probs, v, preferred_element_type=F32)
+            s = lax.dot_general(k, q4, (((1,), (1,)), ((), ())), preferred_element_type=F32)
+            e = jnp.exp(s - jnp.max(s, axis=0, keepdims=True))
+            probs = (e / jnp.sum(e, axis=0, keepdims=True)).astype(BF16)
+            r = lax.dot_general(probs, v, (((0,), (0,)), ((), ())), preferred_element_type=F32)
             o = r[3 * TOK :]
             for h in (2, 1, 0):
                 o = jnp.where(lane_head == h, r[h * TOK : (h + 1) * TOK], o)
@@ -370,7 +397,7 @@
             found += jnp.where(rank_t[k : k + 1, :] == slot, val_t[k : k + 1, :], 0)
         col = jnp.sum(found.astype(F32), axis=1, keepdims=True).astype(jnp.int32)
         slots_v[...] = jnp.broadcast_to(col, (SLOTS, 128))
-        cp = pltpu.make_async_copy(slots_v, slots_s, sems.at[5])
+        cp = pltpu.make_async_copy(slots_v, slots_s, sems.at[7])
         cp.start()
         cp.wait()
         here = jnp.minimum(count - base, SLOTS)
@@ -424,9 +451,11 @@
             jax.ShapeDtypeStruct((SIDE, width), BF16),
             jax.ShapeDtypeStruct((SIDE, width), BF16),
         ),
-        in_specs=[smem, smem, vmem, vmem, vmem] + [anym] * 5,
+        in_specs=[smem, smem, vmem] + [anym] * 7,
         out_specs=(vmem, vmem),
         scratch_shapes=[
+            pltpu.VMEM((SIDE, width), BF16),
+            pltpu.VMEM((SIDE, width), BF16),
             pltpu.VMEM((width, width), BF16),
             pltpu.VMEM((width, 2 * width), BF16),
             pltpu.VMEM((width, width), BF16),
@@ -444,7 +473,7 @@
             pltpu.SMEM((SLOTS, 128), jnp.int32),
             pltpu.VMEM((GROUP * TOK, width), F32),
             pltpu.VMEM((GROUP * TOK, width), F32),
-            pltpu.SemaphoreType.DMA((6,)),
+            pltpu.SemaphoreType.DMA((8,)),
         ],
         compiler_params=pltpu.CompilerParams(vmem_limit_bytes=52 * 1024 * 1024),
         name="cell_pairs",
@@ -453,15 +482,17 @@
 
 
 def reduce_kernel(
-    pa_ref,
-    pb_ref,
+    pa_hbm,
+    pb_hbm,
     out_ref,
+    pb,
     ra,
     rsib,
     sb,
     rz,
     tot,
     ry,
+    loc,
     a_send,
     a_recv,
     s_send,
@@ -474,81 +505,140 @@
     o_recv,
 ):
     z, x, c, y = place()
+
+    def rows(s, h):
+        return pl.ds(pl.multiple_of(s * BLK + h * CHUNK, CHUNK), CHUNK)
+
+    def block(s):
+        return pl.ds(pl.multiple_of(s * BLK, BLK), BLK)
+
+    keep = []
+    for t in range(2):
+        cp = pltpu.make_async_copy(pb_hbm.at[block(t * 2 + c)], pb.at[t], loc.at[t])
+        cp.start()
+        keep.append(cp)
+    self_a = x // 2 == c
+    own_a = pltpu.make_async_copy(pa_hbm.at[block((x % 2) * 2 + c)], ra.at[x], loc.at[2])
+
+    @pl.when(self_a)
+    def _():
+        own_a.start()
+
     barrier, n_peers = barrier_all(z, x, c, y)
     pl.semaphore_wait(barrier, n_peers)
     sib = dev(z, x, 1 - c, y)
 
-    def rows(s):
-        return pl.ds(pl.multiple_of(s * BLK, BLK), BLK)
-
-    sib_cps = []
-    for t in range(2):
-        cp = remote(pb_ref.at[rows(t * 2 + 1 - c)], rsib.at[t], s_send.at[t], s_recv.at[t], sib)
-        cp.start()
-        sib_cps.append(cp)
+    sib_cps = {}
+    for h in range(CHUNKS):
+        for t in range(2):
+            i = h * 2 + t
+            sib_cps[i] = remote(
+                pb_hbm.at[rows(t * 2 + 1 - c, h)],
+                rsib.at[t, pl.ds(h * CHUNK, CHUNK)],
+                s_send.at[i],
+                s_recv.at[i],
+                sib,
+            )
+            sib_cps[i].start()
 
     a_cps = []
-    for s in range(4):
-        xt = 2 * c + s // 2
-        here = jnp.logical_and(xt == x, c == s % 2)
-        cp = remote(pa_ref.at[rows(s)], ra.at[x], a_send.at[s], a_recv.at[x], dev(z, xt, s % 2, y))
-        a_cps.append((here, cp))
-
-        @pl.when(jnp.logical_not(here))
-        def _(cp=cp):
-            cp.start()
-
-        @pl.when(here)
-        def _(s=s):
-            ra[x] = pa_ref[rows(s), :]
+    for h in range(CHUNKS):
+        for s in range(4):
+            xt = 2 * c + s // 2
+            here = jnp.logical_and(xt == x, c == s % 2)
+            cp = remote(
+                pa_hbm.at[rows(s, h)],
+                ra.at[x, pl.ds(h * CHUNK, CHUNK)],
+                a_send.at[h * 4 + s],
+                a_recv.at[h * 4 + x],
+                dev(z, xt, s % 2, y),
+            )
+            a_cps.append((here, cp))
+
+            @pl.when(jnp.logical_not(here))
+            def _(cp=cp):
+                cp.start()
 
     j = (z + y) % 4
     z_cps = []
-    for t in range(2):
-        sib_cps[t].wait_recv()
-        total = pb_ref[rows(t * 2 + c), :].astype(F32) + rsib[t].astype(F32)
-        sb[t] = total.astype(BF16)
-        zt = j + 4 * t
-        here = zt == z
-        cp = remote(sb.at[t], rz.at[z // 4], z_send.at[t], z_recv.at[z // 4], dev(zt, x, c, y))
-        z_cps.append((here, cp))
-
-        @pl.when(jnp.logical_not(here))
-        def _(cp=cp):
-            cp.start()
-
-        @pl.when(here)
-        def _(t=t):
-            rz[t] = sb[t]
-
-    for s in range(4):
-        here = jnp.logical_and(s == x, x // 2 == c)
-
-        @pl.when(jnp.logical_not(here))
-        def _(s=s):
-            remote(pa_ref.at[rows(0)], ra.at[s], a_send.at[0], a_recv.at[s], sib).wait_recv()
-
-    total = ra[0].astype(F32) + ra[1].astype(F32) + ra[2].astype(F32) + ra[3].astype(F32)
-    for t in range(2):
-        here = jnp.logical_and(y == 0, z // 4 == t)
-
-        @pl.when(jnp.logical_not(here))
-        def _(t=t):
-            remote(sb.at[t], rz.at[t], z_send.at[0], z_recv.at[t], sib).wait_recv()
-
-    tot[...] = (total + rz[0].astype(F32) + rz[1].astype(F32)).astype(BF16)
-
-    part = BLK // NY
+    for cp in keep:
+        cp.wait()
+    for h in range(CHUNKS):
+        part = pl.ds(h * CHUNK, CHUNK)
+        for t in range(2):
+            sib_cps[h * 2 + t].wait_recv()
+            total = pb[t, part].astype(F32) + rsib[t, part].astype(F32)
+            sb[t, part] = total.astype(BF16)
+            zt = j + 4 * t
+            here = zt == z
+            cp = remote(
+                sb.at[t, part],
+                rz.at[z // 4, part],
+                z_send.at[h * 2 + t],
+                z_recv.at[h * 2 + z // 4],
+                dev(zt, x, c, y),
+            )
+            z_cps.append((here, cp))
+
+            @pl.when(jnp.logical_not(here))
+            def _(cp=cp):
+                cp.start()
+
+            @pl.when(here)
+            def _(t=t, part=part):
+                rz[t, part] = sb[t, part]
+
+    @pl.when(self_a)
+    def _():
+        own_a.wait()
+
+    share = BLK // NY
 
     def y_rows(yy):
-        return pl.ds(pl.multiple_of(yy * part, part), part)
+        return pl.ds(pl.multiple_of(yy * share, share), share)
+
+    for h in range(CHUNKS):
+        part = pl.ds(h * CHUNK, CHUNK)
+        for s in range(4):
+            here = jnp.logical_and(s == x, self_a)
+
+            @pl.when(jnp.logical_not(here))
+            def _(s=s, part=part, h=h):
+                remote(
+                    pa_hbm.at[rows(0, 0)], ra.at[s, part], a_send.at[0], a_recv.at[h * 4 + s], sib
+                ).wait_recv()
+
+        total = (
+            ra[0, part].astype(F32)
+            + ra[1, part].astype(F32)
+            + ra[2, part].astype(F32)
+            + ra[3, part].astype(F32)
+        )
+        for t in range(2):
+            here = jnp.logical_and(y == 0, z // 4 == t)
+
+            @pl.when(jnp.logical_not(here))
+            def _(t=t, part=part, h=h):
+                remote(
+                    sb.at[t, part], rz.at[t, part], z_send.at[0], z_recv.at[h * 2 + t], sib
+                ).wait_recv()
+
+        tot[part] = (total + rz[0, part].astype(F32) + rz[1, part].astype(F32)).astype(BF16)
+        for d in range(1, NY):
+            yt = (y + d) % NY
+
+            @pl.when(yt * CHUNKS // NY == h)
+            def _(d=d, yt=yt):
+                remote(
+                    tot.at[y_rows(yt)], ry.at[d], y_send.at[d], y_recv.at[d], dev(z, x, c, yt)
+                ).start()
 
     y_cps = []
     for d in range(1, NY):
         yt = (y + d) % NY
-        cp = remote(tot.at[y_rows(yt)], ry.at[d], y_send.at[d], y_recv.at[d], dev(z, x, c, yt))
-        cp.start()
-        y_cps.append(cp)
+        y_cps.append(
+            remote(tot.at[y_rows(yt)], ry.at[d], y_send.at[d], y_recv.at[d], dev(z, x, c, yt))
+        )
     mine = tot[y_rows(y), :].astype(F32)
     for d in range(1, NY):
         y_cps[d - 1].wait_recv()
@@ -565,7 +655,7 @@
         piece = out_ref.at[y_rows((y - d + NY) % NY)]
         remote(piece, piece, o_send.at[d], o_recv.at[d], sib).wait_recv()
 
-    for cp in sib_cps + y_cps + o_cps:
+    for cp in list(sib_cps.values()) + y_cps + o_cps:
         cp.wait_send()
     for here, cp in a_cps + z_cps:
 
@@ -581,21 +671,23 @@
     return pl.pallas_call(
         reduce_kernel,
         out_shape=jax.ShapeDtypeStruct((BLK, width), BF16),
-        in_specs=[vmem] * 2,
+        in_specs=[pl.BlockSpec(memory_space=pl.ANY)] * 2,
         out_specs=vmem,
         scratch_shapes=[
+            pltpu.VMEM((2, BLK, width), BF16),
             pltpu.VMEM((4, BLK, width), BF16),
             pltpu.VMEM((2, BLK, width), BF16),
             pltpu.VMEM((2, BLK, width), BF16),
             pltpu.VMEM((2, BLK, width), BF16),
             pltpu.VMEM((BLK, width), BF16),
             pltpu.VMEM((NY, BLK // NY, width), BF16),
-            dma((4,)),
-            dma((4,)),
-            dma((2,)),
-            dma((2,)),
-            dma((2,)),
-            dma((2,)),
+            dma((3,)),
+            dma((4 * CHUNKS,)),
+            dma((4 * CHUNKS,)),
+            dma((2 * CHUNKS,)),
+            dma((2 * CHUNKS,)),
+            dma((2 * CHUNKS,)),
+            dma((2 * CHUNKS,)),
             dma((4,)),
             dma((4,)),
             dma((4,)),
@@ -622,10 +714,12 @@
 ):
     img_dev, tok_count, enc_width = tokens.shape
     z, x, c, y = place()
-    mine = jnp.concatenate(
-        [pair_list[:, 0], pair_list[:, 1], conf_level, jnp.zeros((PAIR_DEV,), jnp.int32)]
-    ).reshape(1, 1, 128)
-    a_blk, b_blk, pairs = gather(tokens.reshape(img_dev * tok_count, enc_width), proj_in, mine)
+    a_blk, b_blk, pairs = gather(
+        tokens.reshape(img_dev * tok_count, enc_width),
+        proj_in,
+        pair_list.T,
+        conf_level.reshape(1, PAIR_DEV),
+    )
     ids = jnp.stack([z * 2 + c, x, (z + y) % 4, 0]).astype(jnp.int32)
     pa, pb = cell(
         ids, conf_table, pairs, a_blk, b_blk, attn_query, attn_keyval, attn_output, mlp_up, mlp_down

time: 111 us -> 103 us (0.928)
  the two profiles are of different devices: /device:TPU:2 before, /device:TPU:1 now
where the time goes in v2:
time: 103 us; the launch traced here: 101 us
  Pallas kernels  93.3 us (91%)
  local copies, waits for them, and re-layouts  7.78 us (8%)
    pallas_call x1, Pallas kernels, reduce_back(): pl.pallas_call(reduce_kernel, out_shape=jax.ShapeDtypeStruct((BLK, width)...  42.7 us
    pallas_call x1, Pallas kernels, gather(): pl.pallas_call(gather_kernel, out_shape=(jax.ShapeDtypeStruct((SIDE, widt...  29.1 us
    pallas_call x1, Pallas kernels, cell(): pl.pallas_call(cell_kernel, out_shape=(jax.ShapeDtypeStruct((SIDE, width)...  21.5 us
    unnamed x17, local copies, waits for them, and re-layouts  7.78 us

profile of v2, /device:TPU:1, one launch (start us, length us, event | category | flops | bytes accessed | tf_op | source)
XLA Modules:
  0.0 101.2 jit_solution(1006925517685364383)
XLA Ops:
  0.0 0.0 copy-start.6
  0.0 0.1 pad_add_fusion.ids_ref
  0.1 0.0 copy-start
  0.1 1.4 %copy-done = bf16[1024,768]{1,0:T(8,128)(2,1)S(1)} copy-done((bf16[1024,768]{1,0:T(8,128)(2,1)S(1)}, bf16[1024,768]{1,0:T(8,128)(2,1)}, u32[]{:S(2)}) %copy-start) | copy-done | bytes 1572888
  1.5 0.0 copy-start.4
  1.5 1.0 copy-done.4
  2.5 0.0 copy-start.5
  2.5 0.7 copy-done.5
  3.2 0.0 copy-start.7
  3.2 0.7 copy-done.7
  3.8 29.1 %gather_blocks.1 = (bf16[768,768]{1,0:T(8,128)(2,1)S(1)}, bf16[768,768]{1,0:T(8,128)(2,1)S(1)}, s32[256,1,128]{2,1,0:T(1,128)S(1)}) custom-call(bf16[192,1024]{1,0:T(8,128)(2,1)S(1)} %bitcast.8, bf16[1024,768]{1,0:T(8,128)(2,1)S(1)} %copy-done, s32[2,32]{1,0:T(2,128)S(1)} %bitcast.9, s32[1,32]{1,0:T(1,128)S(1)} %bitcast.10), custom_call_target="tpu_custom_call" | custom-call | tf_op jit(solution)/shard_map/gather_blocks/pallas_call | solution.py:226
  33.0 0.0 copy-start.1
  33.0 1.0 %copy-done.1 = bf16[768,768]{1,0:T(8,128)(2,1)} copy-done((bf16[768,768]{1,0:T(8,128)(2,1)}, bf16[768,768]{1,0:T(8,128)(2,1)S(1)}, u32[]{:S(2)}) %copy-start.1) | copy-done | bytes 1179672
  34.0 0.0 copy-start.2
  34.0 1.0 %copy-done.2 = bf16[768,768]{1,0:T(8,128)(2,1)} copy-done((bf16[768,768]{1,0:T(8,128)(2,1)}, bf16[768,768]{1,0:T(8,128)(2,1)S(1)}, u32[]{:S(2)}) %copy-start.2) | copy-done | bytes 1179672
  35.0 0.0 copy-done.6
  35.0 21.5 %cell_pairs.1 = (bf16[768,768]{1,0:T(8,128)(2,1)S(1)}, bf16[768,768]{1,0:T(8,128)(2,1)}) custom-call(s32[4]{0:T(128)S(1)} %pad_add_fusion.ids_ref, f32[16]{0:T(128)S(1)} %copy-done.6, s32[256,1,128]{2,1,0:T(1,128)S(1)} %get-tuple-element.10.list_ref, bf16[768,768]{1,0:T(8,128)(2,1)} %copy-done.1, bf16[768,768]{1,0:T(8,128)(2,1)} %copy-done.2, ...), custom_call_target="tpu_custom_call" | custom-call | tf_op jit(solution)/shard_map/cell_pairs/pallas_call | solution.py:448
  56.5 0.0 copy-start.3
  56.5 1.3 %copy-done.3 = bf16[768,768]{1,0:T(8,128)(2,1)S(1)} copy-done((bf16[768,768]{1,0:T(8,128)(2,1)S(1)}, bf16[768,768]{1,0:T(8,128)(2,1)}, u32[]{:S(2)}) %copy-start.3) | copy-done | bytes 1179672
  57.8 42.7 %reduce_back.1 = bf16[192,768]{1,0:T(8,128)(2,1)S(1)} custom-call(bf16[768,768]{1,0:T(8,128)(2,1)S(1)} %get-tuple-element.13.pa_hbm, bf16[768,768]{1,0:T(8,128)(2,1)S(1)} %copy-done.3), custom_call_target="tpu_custom_call" | custom-call | tf_op jit(solution)/shard_map/reduce_back/pallas_call | solution.py:671
  100.5 0.7 copy.12
Async XLA Ops:
  0.0 35.0 %copy-start.6 = (f32[16]{0:T(128)S(1)}, f32[16]{0:T(128)}, u32[]{:S(2)}) copy-start(f32[16]{0:T(128)} %table_ref.1) | copy-start | bytes 196
  0.1 1.4 %copy-start = (bf16[1024,768]{1,0:T(8,128)(2,1)S(1)}, bf16[1024,768]{1,0:T(8,128)(2,1)}, u32[]{:S(2)}) copy-start(bf16[1024,768]{1,0:T(8,128)(2,1)} %proj_hbm.1) | copy-start | bytes 4718596
  1.5 1.0 copy-start.4
  2.5 0.7 copy-start.5
  3.2 0.7 copy-start.7
  33.0 1.0 %copy-start.1 = (bf16[768,768]{1,0:T(8,128)(2,1)}, bf16[768,768]{1,0:T(8,128)(2,1)S(1)}, u32[]{:S(2)}) copy-start(bf16[768,768]{1,0:T(8,128)(2,1)S(1)} %get-tuple-element.11.a_hbm) | copy-start | bytes 3538948
  34.0 1.0 %copy-start.2 = (bf16[768,768]{1,0:T(8,128)(2,1)}, bf16[768,768]{1,0:T(8,128)(2,1)S(1)}, u32[]{:S(2)}) copy-start(bf16[768,768]{1,0:T(8,128)(2,1)S(1)} %get-tuple-element.12.b_hbm) | copy-start | bytes 3538948
  56.5 1.3 %copy-start.3 = (bf16[768,768]{1,0:T(8,128)(2,1)S(1)}, bf16[768,768]{1,0:T(8,128)(2,1)}, u32[]{:S(2)}) copy-start(bf16[768,768]{1,0:T(8,128)(2,1)} %get-tuple-element.14.pb_hbm) | copy-start | bytes 3538948

commit v3 on v2

--- a/solution.py
+++ b/solution.py
@@ -13,10 +13,12 @@
 SIDE = 4 * BLK
 DEVS = NX * NY * NZ * 2
 PAIR_DEV = 32
-GROUP = 8
+GROUP = 16
+HALF = 8
 SLOTS = 64
 CHUNKS = 2
 CHUNK = BLK // CHUNKS
+SHARE = BLK // NY
 MESH = pl.DeviceIdType.MESH
 F32 = jnp.float32
 BF16 = jnp.bfloat16
@@ -42,21 +44,22 @@
     )
 
 
-def peers_of(z, x, c, y):
-    peers = []
-    for d in range(1, 8):
-        k = (x * 2 + c + d) % 8
-        peers.append(dev(z, k // 2, k % 2, y))
-    for d in range(1, NZ):
-        peers.append(dev((z + d) % NZ, x, c, y))
-    for d in range(1, NY):
-        peers.append(dev(z, x, c, (y + d) % NY))
-    return peers
+def row_peers(z, x, c, y):
+    ks = [(x * 2 + c + d) % 8 for d in range(1, 8)]
+    return [dev(z, k // 2, k % 2, y) for k in ks]
+
+
+def z_peers(z, x, c, y):
+    return [dev((z + d) % NZ, x, c, y) for d in range(1, NZ)]
+
+
+def y_peers(z, x, c, y):
+    return [dev(z, x, c, (y + d) % NY) for d in range(1, NY)]
 
 
 def barrier_all(z, x, c, y):
     barrier = pltpu.get_barrier_semaphore()
-    peers = peers_of(z, x, c, y)
+    peers = row_peers(z, x, c, y) + z_peers(z, x, c, y) + y_peers(z, x, c, y)
     for p in peers:
         pl.semaphore_signal(barrier, inc=1, device_id=p, device_id_type=MESH)
     return barrier, len(peers)
@@ -222,7 +225,7 @@
     width = proj_in.shape[1]
     dma = pltpu.SemaphoreType.DMA
     vmem = pl.BlockSpec(memory_space=pltpu.VMEM)
-    anym = pl.BlockSpec(memory_space=pl.ANY)
+    anym = pl.BlockSpec(memory_space=pltpu.HBM)
     return pl.pallas_call(
         gather_kernel,
         out_shape=(
@@ -347,6 +350,19 @@
     val_t[...] = ((a_img & 31) * 32 + (lax.shift_right_logical(b_img, 8) * 16 + (b_img & 15))) * 16 + level
     count = jnp.sum(hit_f).astype(jnp.int32)
 
+    def fetch_slots():
+        return pltpu.make_async_copy(slots_v, slots_s, sems.at[7])
+
+    def select(block):
+        slot = lax.broadcasted_iota(jnp.int32, (SLOTS, DEVS), 0) + block * SLOTS
+        found = jnp.zeros((SLOTS, DEVS), jnp.int32)
+        for k in range(PAIR_DEV):
+            found += jnp.where(rank_t[k : k + 1, :] == slot, val_t[k : k + 1, :], 0)
+        col = jnp.sum(found.astype(F32), axis=1, keepdims=True).astype(jnp.int32)
+        slots_v[...] = jnp.broadcast_to(col, (SLOTS, 128))
+        fetch_slots().start()
+
+    select(0)
     acc_a[...] = jnp.zeros_like(acc_a)
     acc_b[...] = jnp.zeros_like(acc_b)
 
@@ -389,51 +405,55 @@
             out.append(o)
         return jnp.concatenate(out, axis=1)
 
+    def group(first, here, pairs_in):
+        locs = []
+        for i in range(pairs_in):
+            word = slots_s[first + i, 0]
+            a_loc = word // 512
+            b_loc = (word // 16) % 32
+            locs.append((a_loc, b_loc, word % 16))
+            att[pl.ds(i * TOK, TOK), :] = attend(a_loc, b_loc)
+        rows = pl.ds(0, pairs_in * TOK)
+        query = jnp.concatenate([side[a_loc] for a_loc, _, _ in locs], axis=0)
+        hidden = query + jnp.dot(att[rows, :].astype(BF16), wo[...], preferred_element_type=F32)
+        hn = norm(hidden).astype(BF16)
+        u = jnp.dot(hn, up[...], preferred_element_type=F32)
+        ex = (0.5 * u) * (1.0 + lax.erf(u * (0.5**0.5)))
+        ffn[rows, :] = hidden + jnp.dot(
+            ex.astype(BF16), down[...], preferred_element_type=F32
+        )
+        for i in range(pairs_in):
+            a_loc, b_loc, lev = locs[i]
+
+            @pl.when(first + i < here)
+            def _(i=i, a_loc=a_loc, b_loc=b_loc, lev=lev):
+                feature = table_ref[lev] * ffn[pl.ds(i * TOK, TOK), :]
+                feature = feature.astype(BF16).astype(F32)
+                acc_a[a_loc] = acc_a[a_loc] + feature
+                acc_b[b_loc] = acc_b[b_loc] + feature
+
     def slot_block(block, carry):
-        base = block * SLOTS
-        slot = lax.broadcasted_iota(jnp.int32, (SLOTS, DEVS), 0) + base
-        found = jnp.zeros((SLOTS, DEVS), jnp.int32)
-        for k in range(PAIR_DEV):
-            found += jnp.where(rank_t[k : k + 1, :] == slot, val_t[k : k + 1, :], 0)
-        col = jnp.sum(found.astype(F32), axis=1, keepdims=True).astype(jnp.int32)
-        slots_v[...] = jnp.broadcast_to(col, (SLOTS, 128))
-        cp = pltpu.make_async_copy(slots_v, slots_s, sems.at[7])
-        cp.start()
-        cp.wait()
-        here = jnp.minimum(count - base, SLOTS)
-
-        def group(g, carry2):
-            locs = []
-            for i in range(GROUP):
-                word = slots_s[g * GROUP + i, 0]
-                a_loc = word // 512
-                b_loc = (word // 16) % 32
-                locs.append((a_loc, b_loc, word % 16))
-                att[pl.ds(i * TOK, TOK), :] = attend(a_loc, b_loc)
-            query = jnp.concatenate([side[a_loc] for a_loc, _, _ in locs], axis=0)
-            hidden = query + jnp.dot(
-                att[...].astype(BF16), wo[...], preferred_element_type=F32
-            )
-            hn = norm(hidden).astype(BF16)
-            u = jnp.dot(hn, up[...], preferred_element_type=F32)
-            ex = (0.5 * u) * (1.0 + lax.erf(u * (0.5**0.5)))
-            out = hidden + jnp.dot(ex.astype(BF16), down[...], preferred_element_type=F32)
-            ffn[...] = out
-            for i in range(GROUP):
-                a_loc, b_loc, lev = locs[i]
-
-                @pl.when(g * GROUP + i < here)
-                def _(i=i, a_loc=a_loc, b_loc=b_loc, lev=lev):
-                    feature = table_ref[lev] * ffn[pl.ds(i * TOK, TOK), :]
-                    feature = feature.astype(BF16).astype(F32)
-                    acc_a[a_loc] = acc_a[a_loc] + feature
-                    acc_b[b_loc] = acc_b[b_loc] + feature
-
+        here = jnp.minimum(count - block * SLOTS, SLOTS)
+        wide = (here + GROUP - HALF - 1) // GROUP
+
+        def wide_group(g, carry2):
+            group(g * GROUP, here, GROUP)
             return carry2
 
-        lax.fori_loop(0, (here + GROUP - 1) // GROUP, group, 0)
+        lax.fori_loop(0, wide, wide_group, 0)
+
+        @pl.when(wide * GROUP < here)
+        def _():
+            group(wide * GROUP, here, HALF)
+
+        @pl.when((block + 1) * SLOTS < count)
+        def _():
+            select(block + 1)
+            fetch_slots().wait()
+
         return carry
 
+    fetch_slots().wait()
     lax.fori_loop(0, (count + SLOTS - 1) // SLOTS, slot_block, 0)
     pa_ref[...] = acc_a[...].reshape(SIDE, width).astype(BF16)
     pb_ref[...] = acc_b[...].reshape(SIDE, width).astype(BF16)
@@ -443,7 +463,7 @@
     width, ff = up.shape
     vmem = pl.BlockSpec(memory_space=pltpu.VMEM)
     smem = pl.BlockSpec(memory_space=pltpu.SMEM)
-    anym = pl.BlockSpec(memory_space=pl.ANY)
+    anym = pl.BlockSpec(memory_space=pltpu.HBM)
     images = 4 * IMG_DEV
     return pl.pallas_call(
         cell_kernel,
@@ -505,27 +525,44 @@
     o_recv,
 ):
     z, x, c, y = place()
+    self_a = x // 2 == c
+    self_b = y == 0
 
     def rows(s, h):
         return pl.ds(pl.multiple_of(s * BLK + h * CHUNK, CHUNK), CHUNK)
 
     def block(s):
         return pl.ds(pl.multiple_of(s * BLK, BLK), BLK)
+
+    def y_rows(yy):
+        return pl.ds(pl.multiple_of(yy * SHARE, SHARE), SHARE)
 
     keep = []
     for t in range(2):
         cp = pltpu.make_async_copy(pb_hbm.at[block(t * 2 + c)], pb.at[t], loc.at[t])
         cp.start()
         keep.append(cp)
-    self_a = x // 2 == c
     own_a = pltpu.make_async_copy(pa_hbm.at[block((x % 2) * 2 + c)], ra.at[x], loc.at[2])
 
     @pl.when(self_a)
     def _():
         own_a.start()
 
-    barrier, n_peers = barrier_all(z, x, c, y)
-    pl.semaphore_wait(barrier, n_peers)
+    barrier = pltpu.get_barrier_semaphore()
+    for p in row_peers(z, x, c, y) + y_peers(z, x, c, y):
+        pl.semaphore_signal(barrier, inc=1, device_id=p, device_id_type=MESH)
+    for ys in range(NY):
+        for zh in range(2):
+            zs = (z + NZ - ys) % 4 + 4 * zh
+            here = jnp.logical_and(ys == y, zs == z)
+
+            @pl.when(jnp.logical_not(here))
+            def _(zs=zs, ys=ys):
+                pl.semaphore_signal(
+                    barrier, inc=1, device_id=dev(zs, x, c, ys), device_id_type=MESH
+                )
+
+    pl.semaphore_wait(barrier, 7 + NY - 1 + 2 * NY - jnp.where(self_b, 1, 0))
     sib = dev(z, x, 1 - c, y)
 
     sib_cps = {}
@@ -561,6 +598,7 @@
 
     j = (z + y) % 4
     z_cps = []
+    slot = y * 2 + z // 4
     for cp in keep:
         cp.wait()
     for h in range(CHUNKS):
@@ -570,32 +608,29 @@
             total = pb[t, part].astype(F32) + rsib[t, part].astype(F32)
             sb[t, part] = total.astype(BF16)
             zt = j + 4 * t
-            here = zt == z
-            cp = remote(
-                sb.at[t, part],
-                rz.at[z // 4, part],
-                z_send.at[h * 2 + t],
-                z_recv.at[h * 2 + z // 4],
-                dev(zt, x, c, y),
-            )
-            z_cps.append((here, cp))
-
-            @pl.when(jnp.logical_not(here))
-            def _(cp=cp):
-                cp.start()
-
-            @pl.when(here)
-            def _(t=t, part=part):
-                rz[t, part] = sb[t, part]
+            for q in range(h * NY // CHUNKS, (h + 1) * NY // CHUNKS):
+                piece = pl.ds(q * SHARE, SHARE)
+                here = jnp.logical_and(zt == z, q == y)
+                cp = remote(
+                    sb.at[t, piece],
+                    rz.at[slot],
+                    z_send.at[q * 2 + t],
+                    z_recv.at[slot],
+                    dev(zt, x, c, q),
+                )
+                z_cps.append((here, cp))
+
+                @pl.when(jnp.logical_not(here))
+                def _(cp=cp):
+                    cp.start()
+
+                @pl.when(here)
+                def _(t=t, piece=piece):
+                    rz[slot] = sb[t, piece]
 
     @pl.when(self_a)
     def _():
         own_a.wait()
-
-    share = BLK // NY
-
-    def y_rows(yy):
-        return pl.ds(pl.multiple_of(yy * share, share), share)
 
     for h in range(CHUNKS):
         part = pl.ds(h * CHUNK, CHUNK)
@@ -614,16 +649,7 @@
             + ra[2, part].astype(F32)
             + ra[3, part].astype(F32)
         )
-        for t in range(2):
-            here = jnp.logical_and(y == 0, z // 4 == t)
-
-            @pl.when(jnp.logical_not(here))
-            def _(t=t, part=part, h=h):
-                remote(
-                    sb.at[t, part], rz.at[t, part], z_send.at[0], z_recv.at[h * 2 + t], sib
-                ).wait_recv()
-
-        tot[part] = (total + rz[0, part].astype(F32) + rz[1, part].astype(F32)).astype(BF16)
+        tot[part] = total.astype(BF16)
         for d in range(1, NY):
             yt = (y + d) % NY
 
@@ -643,6 +669,19 @@
     for d in range(1, NY):
         y_cps[d - 1].wait_recv()
         mine = mine + ry[d].astype(F32)
+    for ys in range(NY):
+        for zh in range(2):
+            s = ys * 2 + zh
+            here = jnp.logical_and(jnp.logical_and(self_b, ys == 0), z // 4 == zh)
+
+            @pl.when(jnp.logical_not(here))
+            def _(s=s):
+                remote(
+                    sb.at[0, pl.ds(0, SHARE)], rz.at[s], z_send.at[0], z_recv.at[s], sib
+                ).wait_recv()
+
+    for s in range(2 * NY):
+        mine = mine + rz[s].astype(F32)
     out_ref[y_rows(y), :] = mine.astype(BF16)
     o_cps = []
     for d in range(1, NY):
@@ -671,23 +710,23 @@
     return pl.pallas_call(
         reduce_kernel,
         out_shape=jax.ShapeDtypeStruct((BLK, width), BF16),
-        in_specs=[pl.BlockSpec(memory_space=pl.ANY)] * 2,
+        in_specs=[pl.BlockSpec(memory_space=pltpu.HBM)] * 2,
         out_specs=vmem,
         scratch_shapes=[
             pltpu.VMEM((2, BLK, width), BF16),
             pltpu.VMEM((4, BLK, width), BF16),
             pltpu.VMEM((2, BLK, width), BF16),
             pltpu.VMEM((2, BLK, width), BF16),
-            pltpu.VMEM((2, BLK, width), BF16),
+            pltpu.VMEM((2 * NY, SHARE, width), BF16),
             pltpu.VMEM((BLK, width), BF16),
-            pltpu.VMEM((NY, BLK // NY, width), BF16),
+            pltpu.VMEM((NY, SHARE, width), BF16),
             dma((3,)),
             dma((4 * CHUNKS,)),
             dma((4 * CHUNKS,)),
             dma((2 * CHUNKS,)),
             dma((2 * CHUNKS,)),
-            dma((2 * CHUNKS,)),
-            dma((2 * CHUNKS,)),
+            dma((2 * NY,)),
+            dma((2 * NY,)),
             dma((4,)),
             dma((4,)),
             dma((4,)),

time: 103 us -> 96.8 us (0.940); the launches traced: 101 us -> 96.3 us
  Pallas kernels: 93.3 us -> 88.4 us
    pallas_call x1, Pallas kernels: 21.5 us -> 18.7 us  [cell(): pl.pallas_call(cell_kernel, out_shape=(jax.ShapeDtypeStruct((SIDE, width)...]
    pallas_call x1, Pallas kernels: 42.7 us -> 40.6 us  [reduce_back(): pl.pallas_call(reduce_kernel, out_shape=jax.ShapeDtypeStruct((BLK, width)...]
where the time goes in v3:
time: 96.8 us; the launch traced here: 96.3 us
  Pallas kernels  88.4 us (91%)
  local copies, waits for them, and re-layouts  7.78 us (8%)
    pallas_call x1, Pallas kernels, reduce_back(): pl.pallas_call(reduce_kernel, out_shape=jax.ShapeDtypeStruct((BLK, width)...  40.6 us
    pallas_call x1, Pallas kernels, gather(): pl.pallas_call(gather_kernel, out_shape=(jax.ShapeDtypeStruct((SIDE, widt...  29.1 us
    pallas_call x1, Pallas kernels, cell(): pl.pallas_call(cell_kernel, out_shape=(jax.ShapeDtypeStruct((SIDE, width)...  18.7 us
    unnamed x17, local copies, waits for them, and re-layouts  7.78 us

profile of v3, /device:TPU:1, one launch (start us, length us, event | category | flops | bytes accessed | tf_op | source)
XLA Modules:
  0.0 96.3 jit_solution(3162624181527307971)
XLA Ops:
  0.0 0.0 copy-start.6
  0.0 0.1 pad_add_fusion.ids_ref
  0.1 0.0 copy-start
  0.1 1.4 %copy-done = bf16[1024,768]{1,0:T(8,128)(2,1)S(1)} copy-done((bf16[1024,768]{1,0:T(8,128)(2,1)S(1)}, bf16[1024,768]{1,0:T(8,128)(2,1)}, u32[]{:S(2)}) %copy-start) | copy-done | bytes 1572888
  1.5 0.0 copy-start.4
  1.5 1.0 %copy-done.4 = bf16[8,24,1024]{2,1,0:T(8,128)(2,1)S(1)} copy-done((bf16[8,24,1024]{2,1,0:T(8,128)(2,1)S(1)}, bf16[8,24,1024]{2,1,0:T(8,128)(2,1)}, u32[]{:S(2)}) %copy-start.4) | copy-done | bytes 393240
  2.5 0.0 copy-start.5
  2.5 0.7 copy-done.5
  3.2 0.0 copy-start.7
  3.2 0.7 copy-done.7
  3.8 29.1 %gather_blocks.1 = (bf16[768,768]{1,0:T(8,128)(2,1)S(1)}, bf16[768,768]{1,0:T(8,128)(2,1)S(1)}, s32[256,1,128]{2,1,0:T(1,128)S(1)}) custom-call(bf16[192,1024]{1,0:T(8,128)(2,1)S(1)} %bitcast.8, bf16[1024,768]{1,0:T(8,128)(2,1)S(1)} %copy-done, s32[2,32]{1,0:T(2,128)S(1)} %bitcast.9, s32[1,32]{1,0:T(1,128)S(1)} %bitcast.10), custom_call_target="tpu_custom_call" | custom-call | tf_op jit(solution)/shard_map/gather_blocks/pallas_call | solution.py:229
  33.0 0.0 copy-start.1
  33.0 1.0 %copy-done.1 = bf16[768,768]{1,0:T(8,128)(2,1)} copy-done((bf16[768,768]{1,0:T(8,128)(2,1)}, bf16[768,768]{1,0:T(8,128)(2,1)S(1)}, u32[]{:S(2)}) %copy-start.1) | copy-done | bytes 1179672
  34.0 0.0 copy-start.2
  34.0 1.0 %copy-done.2 = bf16[768,768]{1,0:T(8,128)(2,1)} copy-done((bf16[768,768]{1,0:T(8,128)(2,1)}, bf16[768,768]{1,0:T(8,128)(2,1)S(1)}, u32[]{:S(2)}) %copy-start.2) | copy-done | bytes 1179672
  35.0 0.0 copy-done.6
  35.0 18.7 %cell_pairs.1 = (bf16[768,768]{1,0:T(8,128)(2,1)S(1)}, bf16[768,768]{1,0:T(8,128)(2,1)}) custom-call(s32[4]{0:T(128)S(1)} %pad_add_fusion.ids_ref, f32[16]{0:T(128)S(1)} %copy-done.6, s32[256,1,128]{2,1,0:T(1,128)S(1)} %get-tuple-element.10.list_ref, bf16[768,768]{1,0:T(8,128)(2,1)} %copy-done.1, bf16[768,768]{1,0:T(8,128)(2,1)} %copy-done.2, ...), custom_call_target="tpu_custom_call" | custom-call | tf_op jit(solution)/shard_map/cell_pairs/pallas_call | solution.py:468
  53.7 0.0 copy-start.3
  53.7 1.3 %copy-done.3 = bf16[768,768]{1,0:T(8,128)(2,1)S(1)} copy-done((bf16[768,768]{1,0:T(8,128)(2,1)S(1)}, bf16[768,768]{1,0:T(8,128)(2,1)}, u32[]{:S(2)}) %copy-start.3) | copy-done | bytes 1179672
  55.0 40.6 %reduce_back.1 = bf16[192,768]{1,0:T(8,128)(2,1)S(1)} custom-call(bf16[768,768]{1,0:T(8,128)(2,1)S(1)} %get-tuple-element.13.pa_hbm, bf16[768,768]{1,0:T(8,128)(2,1)S(1)} %copy-done.3), custom_call_target="tpu_custom_call" | custom-call | tf_op jit(solution)/shard_map/reduce_back/pallas_call | solution.py:710
  95.6 0.7 copy.12
Async XLA Ops:
  0.0 35.0 %copy-start.6 = (f32[16]{0:T(128)S(1)}, f32[16]{0:T(128)}, u32[]{:S(2)}) copy-start(f32[16]{0:T(128)} %table_ref.1) | copy-start | bytes 196
  0.1 1.4 %copy-start = (bf16[1024,768]{1,0:T(8,128)(2,1)S(1)}, bf16[1024,768]{1,0:T(8,128)(2,1)}, u32[]{:S(2)}) copy-start(bf16[1024,768]{1,0:T(8,128)(2,1)} %proj_hbm.1) | copy-start | bytes 4718596
  1.5 1.0 %copy-start.4 = (bf16[8,24,1024]{2,1,0:T(8,128)(2,1)S(1)}, bf16[8,24,1024]{2,1,0:T(8,128)(2,1)}, u32[]{:S(2)}) copy-start(bf16[8,24,1024]{2,1,0:T(8,128)(2,1)} %param.10) | copy-start | bytes 1179652
  2.5 0.7 copy-start.5
  3.2 0.7 copy-start.7
  33.0 1.0 %copy-start.1 = (bf16[768,768]{1,0:T(8,128)(2,1)}, bf16[768,768]{1,0:T(8,128)(2,1)S(1)}, u32[]{:S(2)}) copy-start(bf16[768,768]{1,0:T(8,128)(2,1)S(1)} %get-tuple-element.11.a_hbm) | copy-start | bytes 3538948
  34.0 1.0 %copy-start.2 = (bf16[768,768]{1,0:T(8,128)(2,1)}, bf16[768,768]{1,0:T(8,128)(2,1)S(1)}, u32[]{:S(2)}) copy-start(bf16[768,768]{1,0:T(8,128)(2,1)S(1)} %get-tuple-element.12.b_hbm) | copy-start | bytes 3538948
  53.7 1.3 %copy-start.3 = (bf16[768,768]{1,0:T(8,128)(2,1)S(1)}, bf16[768,768]{1,0:T(8,128)(2,1)}, u32[]{:S(2)}) copy-start(bf16[768,768]{1,0:T(8,128)(2,1)} %get-tuple-element.14.pb_hbm) | copy-start | bytes 3538948

commit v4 on v3

--- a/solution.py
+++ b/solution.py
@@ -16,8 +16,8 @@
 GROUP = 16
 HALF = 8
 SLOTS = 64
-CHUNKS = 2
-CHUNK = BLK // CHUNKS
+PARTS = 2
+VMEM_ALL = 64 * 1024 * 1024
 SHARE = BLK // NY
 MESH = pl.DeviceIdType.MESH
 F32 = jnp.float32
@@ -68,13 +68,15 @@
 def gather_kernel(
     tok_hbm,
     proj_hbm,
-    pair_ref,
-    level_ref,
+    pair_hbm,
+    level_hbm,
     a_out,
     b_out,
     list_out,
     tok,
     proj,
+    pair_ref,
+    level_ref,
     own,
     a_send,
     a_recv,
@@ -93,9 +95,15 @@
     z, x, c, y = place()
     tok_in = pltpu.make_async_copy(tok_hbm, tok, loc.at[2])
     proj_in = pltpu.make_async_copy(proj_hbm, proj, loc.at[3])
-    tok_in.start()
-    proj_in.start()
+    pair_in = pltpu.make_async_copy(pair_hbm, pair_ref, loc.at[4])
+    level_in = pltpu.make_async_copy(level_hbm, level_ref, loc.at[5])
+    inputs = (pair_in, level_in, tok_in, proj_in)
+    for cp in inputs:
+        cp.start()
     barrier, n_peers = barrier_all(z, x, c, y)
+    for cp in inputs:
+        cp.wait()
+    own[...] = jnp.dot(tok[...], proj[...], preferred_element_type=F32).astype(BF16)
     me8 = x * 2 + c
     row_me = y * 64 + me8 * 8 + z
     list_out[row_me, :, 0:PAIR_DEV] = pair_ref[0:1, :]
@@ -110,9 +118,6 @@
         cp = remote(mine, mine, lz_send.at[d], lz_recv.at[d], dev((z + d) % NZ, x, c, y))
         cp.start()
         lz.append(cp)
-    tok_in.wait()
-    proj_in.wait()
-    own[...] = jnp.dot(tok[...], proj[...], preferred_element_type=F32).astype(BF16)
 
     s_b = (z // 4) * 2 + c
     b_dst = b_out.at[pl.ds(pl.multiple_of(s_b * BLK, BLK), BLK)]
@@ -233,11 +238,13 @@
             jax.ShapeDtypeStruct((SIDE, width), BF16),
             jax.ShapeDtypeStruct((DEVS, 1, 128), jnp.int32),
         ),
-        in_specs=[anym, anym, vmem, vmem],
+        in_specs=[anym] * 4,
         out_specs=(anym, anym, vmem),
         scratch_shapes=[
             pltpu.VMEM(tokens.shape, BF16),
             pltpu.VMEM(proj_in.shape, BF16),
+            pltpu.VMEM(pairs_t.shape, jnp.int32),
+            pltpu.VMEM(levels.shape, jnp.int32),
             pltpu.VMEM((BLK, width), BF16),
             dma((4,)),
             dma((4,)),
@@ -245,7 +252,7 @@
             dma((2,)),
             dma((2,)),
             dma((2,)),
-            dma((4,)),
+            dma((6,)),
             dma((8,)),
             dma((8,)),
             dma((8,)),
@@ -254,7 +261,7 @@
             dma((4,)),
         ],
         compiler_params=pltpu.CompilerParams(
-            collective_id=0, has_side_effects=True, vmem_limit_bytes=32 * 1024 * 1024
+            collective_id=0, has_side_effects=True, vmem_limit_bytes=VMEM_ALL
         ),
         name="gather_blocks",
     )(tokens, proj_in, pairs_t, levels)
@@ -495,7 +502,7 @@
             pltpu.VMEM((GROUP * TOK, width), F32),
             pltpu.SemaphoreType.DMA((8,)),
         ],
-        compiler_params=pltpu.CompilerParams(vmem_limit_bytes=52 * 1024 * 1024),
+        compiler_params=pltpu.CompilerParams(vmem_limit_bytes=VMEM_ALL),
         name="cell_pairs",
         interpret=interpret,
     )(ids, table, pairs, a_blk, b_blk, wq, wkv, wo, up, down)
@@ -528,9 +535,6 @@
     self_a = x // 2 == c
     self_b = y == 0
 
-    def rows(s, h):
-        return pl.ds(pl.multiple_of(s * BLK + h * CHUNK, CHUNK), CHUNK)
-
     def block(s):
         return pl.ds(pl.multiple_of(s * BLK, BLK), BLK)
 
@@ -565,13 +569,18 @@
     pl.semaphore_wait(barrier, 7 + NY - 1 + 2 * NY - jnp.where(self_b, 1, 0))
     sib = dev(z, x, 1 - c, y)
 
+    width = out_ref.shape[1]
+
+    def cols(n):
+        return pl.ds(n * (width // PARTS), width // PARTS)
+
     sib_cps = {}
-    for h in range(CHUNKS):
+    for n in range(PARTS):
         for t in range(2):
-            i = h * 2 + t
+            i = n * 2 + t
             sib_cps[i] = remote(
-                pb_hbm.at[rows(t * 2 + 1 - c, h)],
-                rsib.at[t, pl.ds(h * CHUNK, CHUNK)],
+                pb_hbm.at[block(t * 2 + 1 - c), cols(n)],
+                rsib.at[t, :, cols(n)],
                 s_send.at[i],
                 s_recv.at[i],
                 sib,
@@ -579,15 +588,15 @@
             sib_cps[i].start()
 
     a_cps = []
-    for h in range(CHUNKS):
+    for n in range(PARTS):
         for s in range(4):
             xt = 2 * c + s // 2
             here = jnp.logical_and(xt == x, c == s % 2)
             cp = remote(
-                pa_hbm.at[rows(s, h)],
-                ra.at[x, pl.ds(h * CHUNK, CHUNK)],
-                a_send.at[h * 4 + s],
-                a_recv.at[h * 4 + x],
+                pa_hbm.at[block(s), cols(n)],
+                ra.at[x, :, cols(n)],
+                a_send.at[n * 4 + s],
+                a_recv.at[n * 4 + x],
                 dev(z, xt, s % 2, y),
             )
             a_cps.append((here, cp))
@@ -601,21 +610,20 @@
     slot = y * 2 + z // 4
     for cp in keep:
         cp.wait()
-    for h in range(CHUNKS):
-        part = pl.ds(h * CHUNK, CHUNK)
+    for n in range(PARTS):
         for t in range(2):
-            sib_cps[h * 2 + t].wait_recv()
-            total = pb[t, part].astype(F32) + rsib[t, part].astype(F32)
-            sb[t, part] = total.astype(BF16)
+            sib_cps[n * 2 + t].wait_recv()
+            total = pb[t, :, cols(n)].astype(F32) + rsib[t, :, cols(n)].astype(F32)
+            sb[t, :, cols(n)] = total.astype(BF16)
             zt = j + 4 * t
-            for q in range(h * NY // CHUNKS, (h + 1) * NY // CHUNKS):
+            for q in range(NY):
                 piece = pl.ds(q * SHARE, SHARE)
                 here = jnp.logical_and(zt == z, q == y)
                 cp = remote(
-                    sb.at[t, piece],
-                    rz.at[slot],
-                    z_send.at[q * 2 + t],
-                    z_recv.at[slot],
+                    sb.at[t, piece, cols(n)],
+                    rz.at[slot, :, cols(n)],
+                    z_send.at[n * 8 + q * 2 + t],
+                    z_recv.at[n * 8 + slot],
                     dev(zt, x, c, q),
                 )
                 z_cps.append((here, cp))
@@ -625,76 +633,88 @@
                     cp.start()
 
                 @pl.when(here)
-                def _(t=t, piece=piece):
-                    rz[slot] = sb[t, piece]
+                def _(t=t, piece=piece, n=n):
+                    rz[slot, :, cols(n)] = sb[t, piece, cols(n)]
 
     @pl.when(self_a)
     def _():
         own_a.wait()
 
-    for h in range(CHUNKS):
-        part = pl.ds(h * CHUNK, CHUNK)
+    y_cps = {}
+    for n in range(PARTS):
         for s in range(4):
             here = jnp.logical_and(s == x, self_a)
 
             @pl.when(jnp.logical_not(here))
-            def _(s=s, part=part, h=h):
+            def _(s=s, n=n):
                 remote(
-                    pa_hbm.at[rows(0, 0)], ra.at[s, part], a_send.at[0], a_recv.at[h * 4 + s], sib
+                    pa_hbm.at[block(0), cols(n)],
+                    ra.at[s, :, cols(n)],
+                    a_send.at[0],
+                    a_recv.at[n * 4 + s],
+                    sib,
                 ).wait_recv()
 
         total = (
-            ra[0, part].astype(F32)
-            + ra[1, part].astype(F32)
-            + ra[2, part].astype(F32)
-            + ra[3, part].astype(F32)
+            ra[0, :, cols(n)].astype(F32)
+            + ra[1, :, cols(n)].astype(F32)
+            + ra[2, :, cols(n)].astype(F32)
+            + ra[3, :, cols(n)].astype(F32)
         )
-        tot[part] = total.astype(BF16)
+        tot[:, cols(n)] = total.astype(BF16)
         for d in range(1, NY):
             yt = (y + d) % NY
-
-            @pl.when(yt * CHUNKS // NY == h)
-            def _(d=d, yt=yt):
-                remote(
-                    tot.at[y_rows(yt)], ry.at[d], y_send.at[d], y_recv.at[d], dev(z, x, c, yt)
-                ).start()
-
-    y_cps = []
-    for d in range(1, NY):
-        yt = (y + d) % NY
-        y_cps.append(
-            remote(tot.at[y_rows(yt)], ry.at[d], y_send.at[d], y_recv.at[d], dev(z, x, c, yt))
-        )
-    mine = tot[y_rows(y), :].astype(F32)
-    for d in range(1, NY):
-        y_cps[d - 1].wait_recv()
-        mine = mine + ry[d].astype(F32)
-    for ys in range(NY):
-        for zh in range(2):
-            s = ys * 2 + zh
-            here = jnp.logical_and(jnp.logical_and(self_b, ys == 0), z // 4 == zh)
-
-            @pl.when(jnp.logical_not(here))
-            def _(s=s):
-                remote(
-                    sb.at[0, pl.ds(0, SHARE)], rz.at[s], z_send.at[0], z_recv.at[s], sib
-                ).wait_recv()
-
-    for s in range(2 * NY):
-        mine = mine + rz[s].astype(F32)
-    out_ref[y_rows(y), :] = mine.astype(BF16)
+            cp = remote(
+                tot.at[y_rows(yt), cols(n)],
+                ry.at[d, :, cols(n)],
+                y_send.at[n * 4 + d],
+                y_recv.at[n * 4 + d],
+                dev(z, x, c, yt),
+            )
+            cp.start()
+            y_cps[n * 4 + d] = cp
+
     o_cps = []
-    for d in range(1, NY):
-        yt = (y + d) % NY
-        piece = out_ref.at[y_rows(y)]
-        cp = remote(piece, piece, o_send.at[d], o_recv.at[d], dev(z, x, c, yt))
-        cp.start()
-        o_cps.append(cp)
-    for d in range(1, NY):
-        piece = out_ref.at[y_rows((y - d + NY) % NY)]
-        remote(piece, piece, o_send.at[d], o_recv.at[d], sib).wait_recv()
-
-    for cp in list(sib_cps.values()) + y_cps + o_cps:
+    for n in range(PARTS):
+        mine = tot[y_rows(y), cols(n)].astype(F32)
+        for d in range(1, NY):
+            y_cps[n * 4 + d].wait_recv()
+            mine = mine + ry[d, :, cols(n)].astype(F32)
+        for ys in range(NY):
+            for zh in range(2):
+                s = ys * 2 + zh
+                here = jnp.logical_and(jnp.logical_and(self_b, ys == 0), z // 4 == zh)
+
+                @pl.when(jnp.logical_not(here))
+                def _(s=s, n=n):
+                    remote(
+                        sb.at[0, pl.ds(0, SHARE), cols(n)],
+                        rz.at[s, :, cols(n)],
+                        z_send.at[0],
+                        z_recv.at[n * 8 + s],
+                        sib,
+                    ).wait_recv()
+
+        for s in range(2 * NY):
+            mine = mine + rz[s, :, cols(n)].astype(F32)
+        out_ref[y_rows(y), cols(n)] = mine.astype(BF16)
+        for d in range(1, NY):
+            piece = out_ref.at[y_rows(y), cols(n)]
+            cp = remote(
+                piece,
+                piece,
+                o_send.at[n * 4 + d],
+                o_recv.at[n * 4 + d],
+                dev(z, x, c, (y + d) % NY),
+            )
+            cp.start()
+            o_cps.append(cp)
+    for n in range(PARTS):
+        for d in range(1, NY):
+            piece = out_ref.at[y_rows((y - d + NY) % NY), cols(n)]
+            remote(piece, piece, o_send.at[d], o_recv.at[n * 4 + d], sib).wait_recv()
+
+    for cp in list(sib_cps.values()) + list(y_cps.values()) + o_cps:
         cp.wait_send()
     for here, cp in a_cps + z_cps:
 
@@ -721,19 +741,19 @@
             pltpu.VMEM((BLK, width), BF16),
             pltpu.VMEM((NY, SHARE, width), BF16),
             dma((3,)),
-            dma((4 * CHUNKS,)),
-            dma((4 * CHUNKS,)),
-            dma((2 * CHUNKS,)),
-            dma((2 * CHUNKS,)),
-            dma((2 * NY,)),
-            dma((2 * NY,)),
-            dma((4,)),
-            dma((4,)),
-            dma((4,)),
-            dma((4,)),
+            dma((4 * PARTS,)),
+            dma((4 * PARTS,)),
+            dma((2 * PARTS,)),
+            dma((2 * PARTS,)),
+            dma((8 * PARTS,)),
+            dma((8 * PARTS,)),
+            dma((4 * PARTS,)),
+            dma((4 * PARTS,)),
+            dma((4 * PARTS,)),
+            dma((4 * PARTS,)),
         ],
         compiler_params=pltpu.CompilerParams(
-            collective_id=1, has_side_effects=True, vmem_limit_bytes=32 * 1024 * 1024
+            collective_id=1, has_side_effects=True, vmem_limit_bytes=VMEM_ALL
         ),
         name="reduce_back",
     )(pa, pb)

time: 96.8 us -> 92.8 us (0.959)
  local copies, waits for them, and re-layouts: 7.78 us -> 1.69 us
  Pallas kernels: 88.4 us -> 90.4 us
    unnamed x17 -> x1, local copies, waits for them, and re-layouts: 7.78 us -> 1.69 us
where the time goes in v4:
time: 92.8 us; the launch traced here: 92.6 us
  Pallas kernels  90.4 us (97%)
  local copies, waits for them, and re-layouts  1.69 us (2%)
    pallas_call x1, Pallas kernels, reduce_back(): pl.pallas_call(reduce_kernel, out_shape=jax.ShapeDtypeStruct((BLK, width)...  41.5 us
    pallas_call x1, Pallas kernels, gather(): pl.pallas_call(gather_kernel, out_shape=(jax.ShapeDtypeStruct((SIDE, widt...  29.4 us
    pallas_call x1, Pallas kernels, cell(): pl.pallas_call(cell_kernel, out_shape=(jax.ShapeDtypeStruct((SIDE, width)...  19.5 us

profile of v4, /device:TPU:1, one launch (start us, length us, event | category | flops | bytes accessed | tf_op | source)
XLA Modules:
  0.0 92.6 jit_solution(14250191581868251806)
XLA Ops:
  0.0 0.6 pad_add_fusion.ids_ref
  0.6 29.4 %gather_blocks.1 = (bf16[768,768]{1,0:T(8,128)(2,1)}, bf16[768,768]{1,0:T(8,128)(2,1)}, s32[256,1,128]{2,1,0:T(1,128)}) custom-call(bf16[192,1024]{1,0:T(8,128)(2,1)} %bitcast.8, bf16[1024,768]{1,0:T(8,128)(2,1)} %proj_hbm.1, s32[2,32]{1,0:T(2,128)} %bitcast.9, s32[1,32]{1,0:T(1,128)} %bitcast.10), custom_call_target="tpu_custom_call" | custom-call | tf_op jit(solution)/shard_map/gather_blocks/pallas_call | solution.py:234
  30.0 19.5 %cell_pairs.1 = (bf16[768,768]{1,0:T(8,128)(2,1)}, bf16[768,768]{1,0:T(8,128)(2,1)}) custom-call(s32[4]{0:T(128)} %pad_add_fusion.ids_ref, f32[16]{0:T(128)} %table_ref.1, s32[256,1,128]{2,1,0:T(1,128)} %get-tuple-element.10.list_ref, bf16[768,768]{1,0:T(8,128)(2,1)} %get-tuple-element.11.a_hbm, bf16[768,768]{1,0:T(8,128)(2,1)} %get-tuple-element.12.b_hbm, ...), custom_call_target="tpu_custom_call" | custom-call | tf_op jit(solution)/shard_map/cell_pairs/pallas_call | solution.py:475
  49.5 41.5 %reduce_back.1 = bf16[192,768]{1,0:T(8,128)(2,1)} custom-call(bf16[768,768]{1,0:T(8,128)(2,1)} %get-tuple-element.13.pa_hbm, bf16[768,768]{1,0:T(8,128)(2,1)} %get-tuple-element.14.pb_hbm), custom_call_target="tpu_custom_call" | custom-call | tf_op jit(solution)/shard_map/reduce_back/pallas_call | solution.py:730
  90.9 1.7 %copy.12 = bf16[8,24,768]{2,1,0:T(8,128)(2,1)} copy(bf16[8,24,768]{2,1,0:T(8,128)(2,1)} %bitcast.7) | data formatting | bytes 589824

commit v5 on v4

--- a/solution.py
+++ b/solution.py
@@ -70,20 +70,33 @@
     proj_hbm,
     pair_hbm,
     level_hbm,
-    a_out,
-    b_out,
+    wq_hbm,
+    wkv_hbm,
+    side_out,
+    q_out,
+    k_out,
+    v_out,
     list_out,
     tok,
     proj,
     pair_ref,
     level_ref,
+    wq,
+    wkv,
+    a_out,
+    b_out,
+    q_buf,
+    k_buf,
+    v_buf,
     own,
+    own_n,
     a_send,
     a_recv,
     b_send,
     b_recv,
     f_send,
     f_recv,
+    out_sem,
     loc,
     lx_send,
     lx_recv,
@@ -100,10 +113,18 @@
     inputs = (pair_in, level_in, tok_in, proj_in)
     for cp in inputs:
         cp.start()
+    weights = (
+        pltpu.make_async_copy(wq_hbm, wq, loc.at[6]),
+        pltpu.make_async_copy(wkv_hbm, wkv, loc.at[7]),
+    )
+    for cp in weights:
+        cp.start()
     barrier, n_peers = barrier_all(z, x, c, y)
     for cp in inputs:
         cp.wait()
-    own[...] = jnp.dot(tok[...], proj[...], preferred_element_type=F32).astype(BF16)
+    projected = jnp.dot(tok[...], proj[...], preferred_element_type=F32).astype(BF16)
+    own[...] = projected
+    own_n[...] = norm(projected.astype(F32)).astype(BF16)
     me8 = x * 2 + c
     row_me = y * 64 + me8 * 8 + z
     list_out[row_me, :, 0:PAIR_DEV] = pair_ref[0:1, :]
@@ -124,10 +145,10 @@
     z0 = (z - y + NZ) % NZ
     z1 = (z - y + NZ + 4) % NZ
     self_b = y == 0
-    b1 = remote(own, b_dst, b_send.at[1], b_recv.at[z // 4], dev(z1, x, c, y))
+    b1 = remote(own_n, b_dst, b_send.at[1], b_recv.at[z // 4], dev(z1, x, c, y))
     b1.start()
-    b0 = remote(own, b_dst, b_send.at[0], b_recv.at[z // 4], dev(z0, x, c, y))
-    b0_local = pltpu.make_async_copy(own, b_dst, loc.at[0])
+    b0 = remote(own_n, b_dst, b_send.at[0], b_recv.at[z // 4], dev(z0, x, c, y))
+    b0_local = pltpu.make_async_copy(own_n, b_dst, loc.at[0])
 
     @pl.when(jnp.logical_not(self_b))
     def _():
@@ -176,15 +197,45 @@
         cp.start()
         ly.append(cp)
 
+    for cp in weights:
+        cp.wait()
+    width = own.shape[1]
     sib = dev(z, x, 1 - c, y)
+    outs = []
+
+    def write(src, dst, rows, k):
+        cp = pltpu.make_async_copy(src.at[rows], dst.at[rows], out_sem.at[k])
+        cp.start()
+        outs.append(cp)
+
+    def query_block(s):
+        rows = pl.ds(s * BLK, BLK)
+        arrived = remote(own, a_out.at[rows], a_send.at[0], a_recv.at[s], sib)
+        here = jnp.logical_and(self_a, s_a == s)
+
+        @pl.when(jnp.logical_not(here))
+        def _():
+            arrived.wait_recv()
+
+        @pl.when(here)
+        def _():
+            a0_local.wait()
+
+        write(a_out, side_out, rows, s)
+        qn = norm(a_out[rows, :].astype(F32)).astype(BF16)
+        q = jnp.dot(qn, wq[...], preferred_element_type=F32).astype(BF16)
+        q_buf[rows, :] = q * jnp.asarray(HEAD_DIM**-0.5, BF16)
+        write(q_buf, q_out, rows, 4 + s)
+
     fwd = []
-    for t in range(2):
+
+    def forward(t):
         slot = b_out.at[pl.ds(pl.multiple_of((t * 2 + c) * BLK, BLK), BLK)]
-        arrived = remote(own, slot, b_send.at[t], b_recv.at[t], sib)
+        arrived = remote(own_n, slot, b_send.at[t], b_recv.at[t], sib)
         here = jnp.logical_and(self_b, z // 4 == t)
 
         @pl.when(jnp.logical_not(here))
-        def _(arrived=arrived):
+        def _():
             arrived.wait_recv()
 
         @pl.when(here)
@@ -195,25 +246,31 @@
         cp.start()
         fwd.append(cp)
 
-    for s in range(4):
-        slot = a_out.at[pl.ds(s * BLK, BLK)]
-        arrived = remote(own, slot, a_send.at[0], a_recv.at[s], sib)
-        here = jnp.logical_and(self_a, s_a == s)
-
-        @pl.when(jnp.logical_not(here))
-        def _(arrived=arrived):
-            arrived.wait_recv()
-
-        @pl.when(here)
-        def _():
-            a0_local.wait()
-
+    def memory_block(s, k):
+        rows = pl.ds(pl.multiple_of(s * BLK, BLK), BLK)
+        mn = b_out[rows, :]
+        k_buf[rows, :] = jnp.dot(mn, wkv[:, :width], preferred_element_type=F32).astype(BF16)
+        write(k_buf, k_out, rows, 8 + k)
+        v_buf[rows, :] = jnp.dot(mn, wkv[:, width:], preferred_element_type=F32).astype(BF16)
+        write(v_buf, v_out, rows, 12 + k)
+
+    query_block(0)
+    query_block(1)
+    forward(0)
+    query_block(2)
+    query_block(3)
+    forward(1)
+    memory_block(c, 0)
+    memory_block(2 + c, 1)
     for t in range(2):
         slot = b_out.at[pl.ds(pl.multiple_of((t * 2 + 1 - c) * BLK, BLK), BLK)]
         remote(slot, slot, f_send.at[t], f_recv.at[t], sib).wait_recv()
+        memory_block(t * 2 + 1 - c, 2 + t)
     for cp in ly:
         cp.wait_recv()
 
+    for cp in outs:
+        cp.wait()
     for cp in lx + lz + ly + a_cps + fwd + [b1]:
         cp.wait_send()
 
@@ -226,7 +283,7 @@
         a0.wait_send()
 
 
-def gather(tokens, proj_in, pairs_t, levels):
+def gather(tokens, proj_in, pairs_t, levels, wq, wkv):
     width = proj_in.shape[1]
     dma = pltpu.SemaphoreType.DMA
     vmem = pl.BlockSpec(memory_space=pltpu.VMEM)
@@ -236,15 +293,25 @@
         out_shape=(
             jax.ShapeDtypeStruct((SIDE, width), BF16),
             jax.ShapeDtypeStruct((SIDE, width), BF16),
+            jax.ShapeDtypeStruct((SIDE, width), BF16),
+            jax.ShapeDtypeStruct((SIDE, width), BF16),
             jax.ShapeDtypeStruct((DEVS, 1, 128), jnp.int32),
         ),
-        in_specs=[anym] * 4,
-        out_specs=(anym, anym, vmem),
+        in_specs=[anym] * 6,
+        out_specs=(anym, anym, anym, anym, vmem),
         scratch_shapes=[
             pltpu.VMEM(tokens.shape, BF16),
             pltpu.VMEM(proj_in.shape, BF16),
             pltpu.VMEM(pairs_t.shape, jnp.int32),
             pltpu.VMEM(levels.shape, jnp.int32),
+            pltpu.VMEM(wq.shape, BF16),
+            pltpu.VMEM(wkv.shape, BF16),
+            pltpu.VMEM((SIDE, width), BF16),
+            pltpu.VMEM((SIDE, width), BF16),
+            pltpu.VMEM((SIDE, width), BF16),
+            pltpu.VMEM((SIDE, width), BF16),
+            pltpu.VMEM((SIDE, width), BF16),
+            pltpu.VMEM((BLK, width), BF16),
             pltpu.VMEM((BLK, width), BF16),
             dma((4,)),
             dma((4,)),
@@ -252,7 +319,8 @@
             dma((2,)),
             dma((2,)),
             dma((2,)),
-            dma((6,)),
+            dma((16,)),
+            dma((8,)),
             dma((8,)),
             dma((8,)),
             dma((8,)),
@@ -264,7 +332,7 @@
             collective_id=0, has_side_effects=True, vmem_limit_bytes=VMEM_ALL
         ),
         name="gather_blocks",
-    )(tokens, proj_in, pairs_t, levels)
+    )(tokens, proj_in, pairs_t, levels, wq, wkv)
 
 
 def norm(v):
@@ -274,22 +342,21 @@
 
 
 def cell_kernel(
-    ids_ref,
     table_ref,
     list_ref,
-    a_hbm,
-    b_hbm,
-    wq_hbm,
-    wkv_hbm,
+    side_hbm,
+    q_hbm,
+    k_hbm,
+    v_hbm,
     wo_hbm,
     up_hbm,
     down_hbm,
     pa_ref,
     pb_ref,
-    a_ref,
-    b_ref,
-    wq,
-    wkv,
+    side_in,
+    q_in,
+    k_in,
+    v_in,
     wo,
     up,
     down,
@@ -307,17 +374,17 @@
     ffn,
     sems,
 ):
-    width = wq.shape[0]
+    width = wo.shape[0]
     heads_quad = 4
     quad = heads_quad * HEAD_DIM
     copies = [
         pltpu.make_async_copy(h, v, sems.at[i])
         for i, (h, v) in enumerate(
             (
-                (a_hbm, a_ref),
-                (wq_hbm, wq),
-                (b_hbm, b_ref),
-                (wkv_hbm, wkv),
+                (q_hbm, q_in),
+                (k_hbm, k_in),
+                (v_hbm, v_in),
+                (side_hbm, side_in),
                 (wo_hbm, wo),
                 (up_hbm, up),
                 (down_hbm, down),
@@ -327,7 +394,8 @@
     for cp in copies:
         cp.start()
 
-    a_id, b_x, b_j = ids_ref[0], ids_ref[1], ids_ref[2]
+    z, x, c, y = place()
+    a_id, b_x, b_j = z * 2 + c, x, (z + y) % 4
     flat = list_ref[...].reshape(DEVS, 128)
     flat_t = flat.astype(F32).T.astype(jnp.int32)
     a_img = flat_t[:PAIR_DEV]
@@ -373,20 +441,9 @@
     acc_a[...] = jnp.zeros_like(acc_a)
     acc_b[...] = jnp.zeros_like(acc_b)
 
-    for cp in copies[:4]:
+    for cp, src, dst in zip(copies, (q_in, k_in, v_in, side_in), (qs, ks, vs, side)):
         cp.wait()
-    for i in range(4):
-        rows = pl.ds(i * BLK, BLK)
-        q_side = a_ref[rows, :].astype(F32)
-        side[pl.ds(i * IMG_DEV, IMG_DEV)] = q_side.reshape(IMG_DEV, TOK, width)
-        qn = norm(q_side).astype(BF16)
-        q = jnp.dot(qn, wq[...], preferred_element_type=F32).astype(BF16).astype(F32)
-        qs[pl.ds(i * IMG_DEV, IMG_DEV)] = (q * (HEAD_DIM**-0.5)).reshape(IMG_DEV, TOK, width)
-        mn = norm(b_ref[rows, :].astype(F32)).astype(BF16)
-        k = jnp.dot(mn, wkv[:, :width], preferred_element_type=F32)
-        ks[pl.ds(i * IMG_DEV, IMG_DEV)] = k.reshape(IMG_DEV, TOK, width)
-        v = jnp.dot(mn, wkv[:, width:], preferred_element_type=F32)
-        vs[pl.ds(i * IMG_DEV, IMG_DEV)] = v.reshape(IMG_DEV, TOK, width)
+        dst[...] = src[...].astype(F32).reshape(dst.shape)
     for cp in copies[4:]:
         cp.wait()
 
@@ -466,7 +523,7 @@
     pb_ref[...] = acc_b[...].reshape(SIDE, width).astype(BF16)
 
 
-def cell(ids, table, pairs, a_blk, b_blk, wq, wkv, wo, up, down, interpret=False):
+def cell(table, pairs, side, q, k, v, wo, up, down):
     width, ff = up.shape
     vmem = pl.BlockSpec(memory_space=pltpu.VMEM)
     smem = pl.BlockSpec(memory_space=pltpu.SMEM)
@@ -478,13 +535,13 @@
             jax.ShapeDtypeStruct((SIDE, width), BF16),
             jax.ShapeDtypeStruct((SIDE, width), BF16),
         ),
-        in_specs=[smem, smem, vmem] + [anym] * 7,
+        in_specs=[smem, vmem] + [anym] * 7,
         out_specs=(vmem, vmem),
         scratch_shapes=[
             pltpu.VMEM((SIDE, width), BF16),
             pltpu.VMEM((SIDE, width), BF16),
-            pltpu.VMEM((width, width), BF16),
-            pltpu.VMEM((width, 2 * width), BF16),
+            pltpu.VMEM((SIDE, width), BF16),
+            pltpu.VMEM((SIDE, width), BF16),
             pltpu.VMEM((width, width), BF16),
             pltpu.VMEM((width, ff), BF16),
             pltpu.VMEM((ff, width), BF16),
@@ -504,8 +561,7 @@
         ],
         compiler_params=pltpu.CompilerParams(vmem_limit_bytes=VMEM_ALL),
         name="cell_pairs",
-        interpret=interpret,
-    )(ids, table, pairs, a_blk, b_blk, wq, wkv, wo, up, down)
+    )(table, pairs, side, q, k, v, wo, up, down)
 
 
 def reduce_kernel(
@@ -753,7 +809,7 @@
             dma((4 * PARTS,)),
         ],
         compiler_params=pltpu.CompilerParams(
-            collective_id=1, has_side_effects=True, vmem_limit_bytes=VMEM_ALL
+            collective_id=1, has_side_effects=True, vmem_limit_bytes=VMEM_ALL - 640 * 1024
         ),
         name="reduce_back",
     )(pa, pb)
@@ -772,17 +828,15 @@
     conf_table,
 ):
     img_dev, tok_count, enc_width = tokens.shape
-    z, x, c, y = place()
-    a_blk, b_blk, pairs = gather(
+    side, q, k, v, pairs = gather(
         tokens.reshape(img_dev * tok_count, enc_width),
         proj_in,
         pair_list.T,
         conf_level.reshape(1, PAIR_DEV),
+        attn_query,
+        attn_keyval,
     )
-    ids = jnp.stack([z * 2 + c, x, (z + y) % 4, 0]).astype(jnp.int32)
-    pa, pb = cell(
-        ids, conf_table, pairs, a_blk, b_blk, attn_query, attn_keyval, attn_output, mlp_up, mlp_down
-    )
+    pa, pb = cell(conf_table, pairs, side, q, k, v, attn_output, mlp_up, mlp_down)
     joined = reduce_back(pa, pb)
     return joined.reshape(img_dev, tok_count, joined.shape[1])
 

time: 92.8 us -> 91.6 us (0.987)
  the two profiles are of different devices: /device:TPU:1 before, /device:TPU:4 now
where the time goes in v5:
time: 91.6 us; the launch traced here: 91.4 us
  Pallas kernels  89.7 us (98%)
  local copies, waits for them, and re-layouts  1.69 us (2%)
    pallas_call x1, Pallas kernels, reduce_back(): pl.pallas_call(reduce_kernel, out_shape=jax.ShapeDtypeStruct((BLK, width)...  40.9 us
    pallas_call x1, Pallas kernels, gather(): pl.pallas_call(gather_kernel, out_shape=(jax.ShapeDtypeStruct((SIDE, widt...  30.9 us
    pallas_call x1, Pallas kernels, cell(): pl.pallas_call(cell_kernel, out_shape=(jax.ShapeDtypeStruct((SIDE, width)...  17.9 us

profile of v5, /device:TPU:4, one launch (start us, length us, event | category | flops | bytes accessed | tf_op | source)
XLA Modules:
  0.0 91.4 jit_solution(14183466057868250082)
XLA Ops:
  0.0 30.9 %gather_blocks.1 = (bf16[768,768]{1,0:T(8,128)(2,1)}, bf16[768,768]{1,0:T(8,128)(2,1)}, bf16[768,768]{1,0:T(8,128)(2,1)}, bf16[768,768]{1,0:T(8,128)(2,1)}, s32[256,1,128]{2,1,0:T(1,128)}) custom-call(bf16[192,1024]{1,0:T(8,128)(2,1)} %bitcast.5, bf16[1024,768]{1,0:T(8,128)(2,1)} %proj_hbm.1, s32[2,32]{1,0:T(2,128)} %bitcast.6, s32[1,32]{1,0:T(1,128)} %bitcast.7, ...), custom_call_target="tpu_custom_call" | custom-call | tf_op jit(solution)/shard_map/gather_blocks/pallas_call | solution.py:291
  30.9 17.9 %cell_pairs.1 = (bf16[768,768]{1,0:T(8,128)(2,1)}, bf16[768,768]{1,0:T(8,128)(2,1)}) custom-call(f32[16]{0:T(128)} %table_ref.1, s32[256,1,128]{2,1,0:T(1,128)} %get-tuple-element.12.list_ref, bf16[768,768]{1,0:T(8,128)(2,1)} %get-tuple-element.13.side_hbm, bf16[768,768]{1,0:T(8,128)(2,1)} %get-tuple-element.14.q_hbm, ...), custom_call_target="tpu_custom_call" | custom-call | tf_op jit(solution)/shard_map/cell_pairs/pallas_call | solution.py:532
  48.8 40.9 %reduce_back.1 = bf16[192,768]{1,0:T(8,128)(2,1)} custom-call(bf16[768,768]{1,0:T(8,128)(2,1)} %get-tuple-element.17.pa_hbm, bf16[768,768]{1,0:T(8,128)(2,1)} %get-tuple-element.18.pb_hbm), custom_call_target="tpu_custom_call" | custom-call | tf_op jit(solution)/shard_map/reduce_back/pallas_call | solution.py:786
  89.7 1.7 %copy.12 = bf16[8,24,768]{2,1,0:T(8,128)(2,1)} copy(bf16[8,24,768]{2,1,0:T(8,128)(2,1)} %bitcast.4) | data formatting | bytes 589824

commit v6 on v4

--- a/solution.py
+++ b/solution.py
@@ -19,6 +19,7 @@
 PARTS = 2
 VMEM_ALL = 64 * 1024 * 1024
 SHARE = BLK // NY
+FAR = 128
 MESH = pl.DeviceIdType.MESH
 F32 = jnp.float32
 BF16 = jnp.bfloat16
@@ -63,6 +64,14 @@
     for p in peers:
         pl.semaphore_signal(barrier, inc=1, device_id=p, device_id_type=MESH)
     return barrier, len(peers)
+
+
+def far_target(z, y):
+    return (z + jnp.where(y == 1, 3, 5)) % NZ
+
+
+def far_source(z, y):
+    return (z + jnp.where(y == 1, 5, 3)) % NZ
 
 
 def gather_kernel(
@@ -101,6 +110,14 @@
     for cp in inputs:
         cp.start()
     barrier, n_peers = barrier_all(z, x, c, y)
+    odd = y % 2 == 1
+    other = (y + 2) % NY
+
+    @pl.when(odd)
+    def _():
+        source = dev(far_source(z, y), x, c, other)
+        pl.semaphore_signal(barrier, inc=1, device_id=source, device_id_type=MESH)
+
     for cp in inputs:
         cp.wait()
     own[...] = jnp.dot(tok[...], proj[...], preferred_element_type=F32).astype(BF16)
@@ -110,7 +127,7 @@
     list_out[row_me, :, PAIR_DEV : 2 * PAIR_DEV] = pair_ref[1:2, :]
     list_out[row_me, :, 2 * PAIR_DEV : 3 * PAIR_DEV] = level_ref[...]
     list_out[row_me, :, 3 * PAIR_DEV :] = jnp.zeros((1, 128 - 3 * PAIR_DEV), jnp.int32)
-    pl.semaphore_wait(barrier, n_peers)
+    pl.semaphore_wait(barrier, n_peers + jnp.where(odd, 1, 0))
 
     lz = []
     for d in range(1, NZ):
@@ -124,18 +141,31 @@
     z0 = (z - y + NZ) % NZ
     z1 = (z - y + NZ + 4) % NZ
     self_b = y == 0
-    b1 = remote(own, b_dst, b_send.at[1], b_recv.at[z // 4], dev(z1, x, c, y))
-    b1.start()
-    b0 = remote(own, b_dst, b_send.at[0], b_recv.at[z // 4], dev(z0, x, c, y))
     b0_local = pltpu.make_async_copy(own, b_dst, loc.at[0])
-
-    @pl.when(jnp.logical_not(self_b))
-    def _():
-        b0.start()
 
     @pl.when(self_b)
     def _():
         b0_local.start()
+
+    near_dst = b_out.at[pl.ds(pl.multiple_of(s_b * BLK, BLK), FAR)]
+    far_dst = b_out.at[pl.ds(pl.multiple_of(s_b * BLK + FAR, BLK - FAR), BLK - FAR)]
+    over = dev(far_target(z, other), x, c, other)
+    cross = remote(own.at[pl.ds(FAR, BLK - FAR)], far_dst, b_send.at[2], b_recv.at[2], over)
+    b_cps = [(odd, cross)]
+    for t, zt in ((1, z1), (0, z0)):
+        far = y == (1 if t == 1 else 3)
+        whole = remote(own, b_dst, b_send.at[t], b_recv.at[z // 4], dev(zt, x, c, y))
+        most = remote(
+            own.at[pl.ds(0, FAR)], near_dst, b_send.at[t], b_recv.at[z // 4], dev(zt, x, c, y)
+        )
+        b_cps.append((far, most))
+        full = jnp.logical_not(far)
+        b_cps.append((jnp.logical_and(full, jnp.logical_not(self_b)) if t == 0 else full, whole))
+    for go, cp in b_cps:
+
+        @pl.when(go)
+        def _(cp=cp):
+            cp.start()
 
     for cp in lz:
         cp.wait_recv()
@@ -179,13 +209,34 @@
     sib = dev(z, x, 1 - c, y)
     fwd = []
     for t in range(2):
-        slot = b_out.at[pl.ds(pl.multiple_of((t * 2 + c) * BLK, BLK), BLK)]
+        base = (t * 2 + c) * BLK
+        slot = b_out.at[pl.ds(pl.multiple_of(base, BLK), BLK)]
         arrived = remote(own, slot, b_send.at[t], b_recv.at[t], sib)
+        most = remote(
+            own.at[pl.ds(0, FAR)],
+            b_out.at[pl.ds(pl.multiple_of(base, BLK), FAR)],
+            b_send.at[t],
+            b_recv.at[t],
+            sib,
+        )
+        rest = remote(
+            own.at[pl.ds(FAR, BLK - FAR)],
+            b_out.at[pl.ds(pl.multiple_of(base + FAR, BLK - FAR), BLK - FAR)],
+            b_send.at[2],
+            b_recv.at[2],
+            sib,
+        )
         here = jnp.logical_and(self_b, z // 4 == t)
-
-        @pl.when(jnp.logical_not(here))
+        split = jnp.logical_and(odd, far_source(z, y) // 4 == t)
+
+        @pl.when(jnp.logical_not(jnp.logical_or(here, split)))
         def _(arrived=arrived):
             arrived.wait_recv()
+
+        @pl.when(split)
+        def _(most=most, rest=rest):
+            most.wait_recv()
+            rest.wait_recv()
 
         @pl.when(here)
         def _():
@@ -214,12 +265,14 @@
     for cp in ly:
         cp.wait_recv()
 
-    for cp in lx + lz + ly + a_cps + fwd + [b1]:
+    for cp in lx + lz + ly + a_cps + fwd:
         cp.wait_send()
 
-    @pl.when(jnp.logical_not(self_b))
-    def _():
-        b0.wait_send()
+    for go, cp in b_cps:
+
+        @pl.when(go)
+        def _(cp=cp):
+            cp.wait_send()
 
     @pl.when(jnp.logical_not(self_a))
     def _():
@@ -248,8 +301,8 @@
             pltpu.VMEM((BLK, width), BF16),
             dma((4,)),
             dma((4,)),
-            dma((2,)),
-            dma((2,)),
+            dma((3,)),
+            dma((3,)),
             dma((2,)),
             dma((2,)),
             dma((6,)),
@@ -274,7 +327,6 @@
 
 
 def cell_kernel(
-    ids_ref,
     table_ref,
     list_ref,
     a_hbm,
@@ -327,7 +379,8 @@
     for cp in copies:
         cp.start()
 
-    a_id, b_x, b_j = ids_ref[0], ids_ref[1], ids_ref[2]
+    z, x, c, y = place()
+    a_id, b_x, b_j = z * 2 + c, x, (z + y) % 4
     flat = list_ref[...].reshape(DEVS, 128)
     flat_t = flat.astype(F32).T.astype(jnp.int32)
     a_img = flat_t[:PAIR_DEV]
@@ -466,7 +519,7 @@
     pb_ref[...] = acc_b[...].reshape(SIDE, width).astype(BF16)
 
 
-def cell(ids, table, pairs, a_blk, b_blk, wq, wkv, wo, up, down, interpret=False):
+def cell(table, pairs, a_blk, b_blk, wq, wkv, wo, up, down):
     width, ff = up.shape
     vmem = pl.BlockSpec(memory_space=pltpu.VMEM)
     smem = pl.BlockSpec(memory_space=pltpu.SMEM)
@@ -478,7 +531,7 @@
             jax.ShapeDtypeStruct((SIDE, width), BF16),
             jax.ShapeDtypeStruct((SIDE, width), BF16),
         ),
-        in_specs=[smem, smem, vmem] + [anym] * 7,
+        in_specs=[smem, vmem] + [anym] * 7,
         out_specs=(vmem, vmem),
         scratch_shapes=[
             pltpu.VMEM((SIDE, width), BF16),
@@ -504,8 +557,7 @@
         ],
         compiler_params=pltpu.CompilerParams(vmem_limit_bytes=VMEM_ALL),
         name="cell_pairs",
-        interpret=interpret,
-    )(ids, table, pairs, a_blk, b_blk, wq, wkv, wo, up, down)
+    )(table, pairs, a_blk, b_blk, wq, wkv, wo, up, down)
 
 
 def reduce_kernel(
@@ -772,16 +824,14 @@
     conf_table,
 ):
     img_dev, tok_count, enc_width = tokens.shape
-    z, x, c, y = place()
     a_blk, b_blk, pairs = gather(
         tokens.reshape(img_dev * tok_count, enc_width),
         proj_in,
         pair_list.T,
         conf_level.reshape(1, PAIR_DEV),
     )
-    ids = jnp.stack([z * 2 + c, x, (z + y) % 4, 0]).astype(jnp.int32)
     pa, pb = cell(
-        ids, conf_table, pairs, a_blk, b_blk, attn_query, attn_keyval, attn_output, mlp_up, mlp_down
+        conf_table, pairs, a_blk, b_blk, attn_query, attn_keyval, attn_output, mlp_up, mlp_down
     )
     joined = reduce_back(pa, pb)
     return joined.reshape(img_dev, tok_count, joined.shape[1])

time: 92.8 us -> 87.4 us (0.942); the launches traced: 92.6 us -> 86 us
  Pallas kernels: 90.4 us -> 84.2 us
    pallas_call x1, Pallas kernels: 41.5 us -> 35.2 us  [reduce_back(): pl.pallas_call(reduce_kernel, out_shape=jax.ShapeDtypeStruct((BLK, width)...]
where the time goes in v6:
time: 87.4 us; the launch traced here: 86 us
  Pallas kernels  84.2 us (96%)
  local copies, waits for them, and re-layouts  1.69 us (2%)
    pallas_call x1, Pallas kernels, reduce_back(): pl.pallas_call(reduce_kernel, out_shape=jax.ShapeDtypeStruct((BLK, width)...  35.2 us
    pallas_call x1, Pallas kernels, gather(): pl.pallas_call(gather_kernel, out_shape=(jax.ShapeDtypeStruct((SIDE, widt...  29.5 us
    pallas_call x1, Pallas kernels, cell(): pl.pallas_call(cell_kernel, out_shape=(jax.ShapeDtypeStruct((SIDE, width)...  19.5 us

profile of v6, /device:TPU:1, one launch (start us, length us, event | category | flops | bytes accessed | tf_op | source)
XLA Modules:
  0.0 86.0 jit_solution(4440943091715776330)
XLA Ops:
  0.0 29.5 %gather_blocks.1 = (bf16[768,768]{1,0:T(8,128)(2,1)}, bf16[768,768]{1,0:T(8,128)(2,1)}, s32[256,1,128]{2,1,0:T(1,128)}) custom-call(bf16[192,1024]{1,0:T(8,128)(2,1)} %bitcast.5, bf16[1024,768]{1,0:T(8,128)(2,1)} %proj_hbm.1, s32[2,32]{1,0:T(2,128)} %bitcast.6, s32[1,32]{1,0:T(1,128)} %bitcast.7), custom_call_target="tpu_custom_call" | custom-call | tf_op jit(solution)/shard_map/gather_blocks/pallas_call | solution.py:287
  29.5 19.5 %cell_pairs.1 = (bf16[768,768]{1,0:T(8,128)(2,1)}, bf16[768,768]{1,0:T(8,128)(2,1)}) custom-call(f32[16]{0:T(128)} %table_ref.1, s32[256,1,128]{2,1,0:T(1,128)} %get-tuple-element.10.list_ref, bf16[768,768]{1,0:T(8,128)(2,1)} %get-tuple-element.11.a_hbm, bf16[768,768]{1,0:T(8,128)(2,1)} %get-tuple-element.12.b_hbm, bf16[768,768]{1,0:T(8,128)(2,1)} %wq_hbm.1, ...), custom_call_target="tpu_custom_call" | custom-call | tf_op jit(solution)/shard_map/cell_pairs/pallas_call | solution.py:528
  49.0 35.2 %reduce_back.1 = bf16[192,768]{1,0:T(8,128)(2,1)} custom-call(bf16[768,768]{1,0:T(8,128)(2,1)} %get-tuple-element.13.pa_hbm, bf16[768,768]{1,0:T(8,128)(2,1)} %get-tuple-element.14.pb_hbm), custom_call_target="tpu_custom_call" | custom-call | tf_op jit(solution)/shard_map/reduce_back/pallas_call | solution.py:782
  84.3 1.7 %copy.12 = bf16[8,24,768]{2,1,0:T(8,128)(2,1)} copy(bf16[8,24,768]{2,1,0:T(8,128)(2,1)} %bitcast.4) | data formatting | bytes 589824

commit v7 on v6

--- a/solution.py
+++ b/solution.py
@@ -571,6 +571,8 @@
     rz,
     tot,
     ry,
+    rx,
+    relay,
     loc,
     a_send,
     a_recv,
@@ -582,6 +584,9 @@
     y_recv,
     o_send,
     o_recv,
+    x_send,
+    x_recv,
+    h_send,
 ):
     z, x, c, y = place()
     self_a = x // 2 == c
@@ -618,7 +623,16 @@
                     barrier, inc=1, device_id=dev(zs, x, c, ys), device_id_type=MESH
                 )
 
-    pl.semaphore_wait(barrier, 7 + NY - 1 + 2 * NY - jnp.where(self_b, 1, 0))
+    odd = y % 2 == 1
+    other = (y + 2) % NY
+
+    @pl.when(odd)
+    def _():
+        for p in (dev(z, x, 1 - c, other), dev(far_target(z, other), x, c, y)):
+            pl.semaphore_signal(barrier, inc=1, device_id=p, device_id_type=MESH)
+
+    extra = jnp.where(odd, 2, jnp.where(self_b, -1, 0))
+    pl.semaphore_wait(barrier, 7 + NY - 1 + 2 * NY + extra)
     sib = dev(z, x, 1 - c, y)
 
     width = out_ref.shape[1]
@@ -638,6 +652,25 @@
                 sib,
             )
             sib_cps[i].start()
+
+    far = far_source(z, y)
+    x_cps = []
+    for n in range(PARTS):
+        for cc in range(2):
+            s = (far // 4) * 2 + cc
+            piece = pl.ds(pl.multiple_of(s * BLK + other * SHARE, SHARE), SHARE)
+            cp = remote(
+                pb_hbm.at[piece, cols(n)],
+                rx.at[c, :, cols(n)],
+                x_send.at[n * 2 + cc],
+                x_recv.at[n * 2 + c],
+                dev(z, x, cc, other),
+            )
+            x_cps.append(cp)
+
+            @pl.when(odd)
+            def _(cp=cp):
+                cp.start()
 
     a_cps = []
     for n in range(PARTS):
@@ -678,15 +711,44 @@
                     z_recv.at[n * 8 + slot],
                     dev(zt, x, c, q),
                 )
-                z_cps.append((here, cp))
-
-                @pl.when(jnp.logical_not(here))
+                turn = jnp.logical_and(odd, jnp.logical_and(far // 4 == t, q == other))
+                kept = jnp.logical_or(here, turn)
+                z_cps.append((kept, cp))
+
+                @pl.when(jnp.logical_not(kept))
                 def _(cp=cp):
                     cp.start()
 
                 @pl.when(here)
                 def _(t=t, piece=piece, n=n):
                     rz[slot, :, cols(n)] = sb[t, piece, cols(n)]
+
+    h_slot = other * 2 + z // 4
+    h_cps = []
+    for n in range(PARTS):
+        h_cps.append(
+            remote(
+                relay.at[:, cols(n)],
+                rz.at[h_slot, :, cols(n)],
+                h_send.at[n],
+                z_recv.at[n * 8 + h_slot],
+                dev(far_source(z, other), x, c, y),
+            )
+        )
+
+        @pl.when(odd)
+        def _(n=n):
+            for cc in range(2):
+                remote(
+                    pb_hbm.at[pl.ds(0, SHARE), cols(n)],
+                    rx.at[cc, :, cols(n)],
+                    x_send.at[0],
+                    x_recv.at[n * 2 + cc],
+                    sib,
+                ).wait_recv()
+            both = rx[0, :, cols(n)].astype(F32) + rx[1, :, cols(n)].astype(F32)
+            relay[:, cols(n)] = both.astype(BF16)
+            h_cps[n].start()
 
     @pl.when(self_a)
     def _():
@@ -774,6 +836,12 @@
         def _(cp=cp):
             cp.wait_send()
 
+    for cp in x_cps + h_cps:
+
+        @pl.when(odd)
+        def _(cp=cp):
+            cp.wait_send()
+
 
 def reduce_back(pa, pb):
     width = pa.shape[1]
@@ -792,6 +860,8 @@
             pltpu.VMEM((2 * NY, SHARE, width), BF16),
             pltpu.VMEM((BLK, width), BF16),
             pltpu.VMEM((NY, SHARE, width), BF16),
+            pltpu.VMEM((2, SHARE, width), BF16),
+            pltpu.VMEM((SHARE, width), BF16),
             dma((3,)),
             dma((4 * PARTS,)),
             dma((4 * PARTS,)),
@@ -803,6 +873,9 @@
             dma((4 * PARTS,)),
             dma((4 * PARTS,)),
             dma((4 * PARTS,)),
+            dma((2 * PARTS,)),
+            dma((2 * PARTS,)),
+            dma((PARTS,)),
         ],
         compiler_params=pltpu.CompilerParams(
             collective_id=1, has_side_effects=True, vmem_limit_bytes=VMEM_ALL

time: 87.4 us -> 85.3 us (0.976); the launches traced: 86 us -> 84.9 us
  Pallas kernels: 84.2 us -> 83.2 us
    pallas_call x1, Pallas kernels: 35.2 us -> 34.2 us  [reduce_back(): pl.pallas_call(reduce_kernel, out_shape=jax.ShapeDtypeStruct((BLK, width)...]
where the time goes in v7:
time: 85.3 us; the launch traced here: 84.9 us
  Pallas kernels  83.2 us (98%)
  local copies, waits for them, and re-layouts  1.69 us (2%)
    pallas_call x1, Pallas kernels, reduce_back(): pl.pallas_call(reduce_kernel, out_shape=jax.ShapeDtypeStruct((BLK, width)...  34.2 us
    pallas_call x1, Pallas kernels, gather(): pl.pallas_call(gather_kernel, out_shape=(jax.ShapeDtypeStruct((SIDE, widt...  29.5 us
    pallas_call x1, Pallas kernels, cell(): pl.pallas_call(cell_kernel, out_shape=(jax.ShapeDtypeStruct((SIDE, width)...  19.4 us

profile of v7, /device:TPU:1, one launch (start us, length us, event | category | flops | bytes accessed | tf_op | source)
XLA Modules:
  0.0 84.9 jit_solution(16490622507082885072)
XLA Ops:
  0.0 29.5 %gather_blocks.1 = (bf16[768,768]{1,0:T(8,128)(2,1)}, bf16[768,768]{1,0:T(8,128)(2,1)}, s32[256,1,128]{2,1,0:T(1,128)}) custom-call(bf16[192,1024]{1,0:T(8,128)(2,1)} %bitcast.5, bf16[1024,768]{1,0:T(8,128)(2,1)} %proj_hbm.1, s32[2,32]{1,0:T(2,128)} %bitcast.6, s32[1,32]{1,0:T(1,128)} %bitcast.7), custom_call_target="tpu_custom_call" | custom-call | tf_op jit(solution)/shard_map/gather_blocks/pallas_call | solution.py:287
  29.5 19.4 %cell_pairs.1 = (bf16[768,768]{1,0:T(8,128)(2,1)}, bf16[768,768]{1,0:T(8,128)(2,1)}) custom-call(f32[16]{0:T(128)} %table_ref.1, s32[256,1,128]{2,1,0:T(1,128)} %get-tuple-element.10.list_ref, bf16[768,768]{1,0:T(8,128)(2,1)} %get-tuple-element.11.a_hbm, bf16[768,768]{1,0:T(8,128)(2,1)} %get-tuple-element.12.b_hbm, bf16[768,768]{1,0:T(8,128)(2,1)} %wq_hbm.1, ...), custom_call_target="tpu_custom_call" | custom-call | tf_op jit(solution)/shard_map/cell_pairs/pallas_call | solution.py:528
  49.0 34.2 %reduce_back.1 = bf16[192,768]{1,0:T(8,128)(2,1)} custom-call(bf16[768,768]{1,0:T(8,128)(2,1)} %get-tuple-element.13.pa_hbm, bf16[768,768]{1,0:T(8,128)(2,1)} %get-tuple-element.14.pb_hbm), custom_call_target="tpu_custom_call" | custom-call | tf_op jit(solution)/shard_map/reduce_back/pallas_call | solution.py:850
  83.2 1.7 %copy.12 = bf16[8,24,768]{2,1,0:T(8,128)(2,1)} copy(bf16[8,24,768]{2,1,0:T(8,128)(2,1)} %bitcast.4) | data formatting | bytes 589824

commit v8 on v7

--- a/solution.py
+++ b/solution.py
@@ -13,9 +13,9 @@
 SIDE = 4 * BLK
 DEVS = NX * NY * NZ * 2
 PAIR_DEV = 32
-GROUP = 16
+GROUP = 24
 HALF = 8
-SLOTS = 64
+SLOTS = 72
 PARTS = 2
 VMEM_ALL = 64 * 1024 * 1024
 SHARE = BLK // NY
@@ -328,7 +328,7 @@
 
 def cell_kernel(
     table_ref,
-    list_ref,
+    list_hbm,
     a_hbm,
     b_hbm,
     wq_hbm,
@@ -336,8 +336,9 @@
     wo_hbm,
     up_hbm,
     down_hbm,
-    pa_ref,
-    pb_ref,
+    pa_hbm,
+    pb_hbm,
+    list_ref,
     a_ref,
     b_ref,
     wq,
@@ -376,8 +377,13 @@
             )
         )
     ]
-    for cp in copies:
+    list_in = pltpu.make_async_copy(list_hbm, list_ref, sems.at[8])
+    list_in.start()
+    for cp in copies[:4]:
         cp.start()
+    acc_a[...] = jnp.zeros_like(acc_a)
+    acc_b[...] = jnp.zeros_like(acc_b)
+    list_in.wait()
 
     z, x, c, y = place()
     a_id, b_x, b_j = z * 2 + c, x, (z + y) % 4
@@ -423,11 +429,11 @@
         fetch_slots().start()
 
     select(0)
-    acc_a[...] = jnp.zeros_like(acc_a)
-    acc_b[...] = jnp.zeros_like(acc_b)
 
     for cp in copies[:4]:
         cp.wait()
+    for cp in copies[4:]:
+        cp.start()
     for i in range(4):
         rows = pl.ds(i * BLK, BLK)
         q_side = a_ref[rows, :].astype(F32)
@@ -515,13 +521,21 @@
 
     fetch_slots().wait()
     lax.fori_loop(0, (count + SLOTS - 1) // SLOTS, slot_block, 0)
-    pa_ref[...] = acc_a[...].reshape(SIDE, width).astype(BF16)
-    pb_ref[...] = acc_b[...].reshape(SIDE, width).astype(BF16)
+    outs = []
+    for i in range(4):
+        rows = pl.ds(i * BLK, BLK)
+        images = pl.ds(i * IMG_DEV, IMG_DEV)
+        for k, (acc, buf, hbm) in enumerate(((acc_a, a_ref, pa_hbm), (acc_b, b_ref, pb_hbm))):
+            buf[rows, :] = acc[images].reshape(BLK, width).astype(BF16)
+            cp = pltpu.make_async_copy(buf.at[rows], hbm.at[rows], sems.at[9 + 2 * i + k])
+            cp.start()
+            outs.append(cp)
+    for cp in outs:
+        cp.wait()
 
 
 def cell(table, pairs, a_blk, b_blk, wq, wkv, wo, up, down):
     width, ff = up.shape
-    vmem = pl.BlockSpec(memory_space=pltpu.VMEM)
     smem = pl.BlockSpec(memory_space=pltpu.SMEM)
     anym = pl.BlockSpec(memory_space=pltpu.HBM)
     images = 4 * IMG_DEV
@@ -531,9 +545,10 @@
             jax.ShapeDtypeStruct((SIDE, width), BF16),
             jax.ShapeDtypeStruct((SIDE, width), BF16),
         ),
-        in_specs=[smem, vmem] + [anym] * 7,
-        out_specs=(vmem, vmem),
+        in_specs=[smem] + [anym] * 8,
+        out_specs=(anym, anym),
         scratch_shapes=[
+            pltpu.VMEM((DEVS, 1, 128), jnp.int32),
             pltpu.VMEM((SIDE, width), BF16),
             pltpu.VMEM((SIDE, width), BF16),
             pltpu.VMEM((width, width), BF16),
@@ -553,7 +568,7 @@
             pltpu.SMEM((SLOTS, 128), jnp.int32),
             pltpu.VMEM((GROUP * TOK, width), F32),
             pltpu.VMEM((GROUP * TOK, width), F32),
-            pltpu.SemaphoreType.DMA((8,)),
+            pltpu.SemaphoreType.DMA((17,)),
         ],
         compiler_params=pltpu.CompilerParams(vmem_limit_bytes=VMEM_ALL),
         name="cell_pairs",
@@ -878,7 +893,7 @@
             dma((PARTS,)),
         ],
         compiler_params=pltpu.CompilerParams(
-            collective_id=1, has_side_effects=True, vmem_limit_bytes=VMEM_ALL
+            collective_id=1, has_side_effects=True, vmem_limit_bytes=VMEM_ALL - 1100 * 1024
         ),
         name="reduce_back",
     )(pa, pb)

time: 85.3 us -> 84.8 us (level)
  no operation moved by 1% of the time
where the time goes in v8:
time: 84.8 us; the launch traced here: 84.4 us
  Pallas kernels  82.7 us (98%)
  local copies, waits for them, and re-layouts  1.69 us (2%)
    pallas_call x1, Pallas kernels, reduce_back(): pl.pallas_call(reduce_kernel, out_shape=jax.ShapeDtypeStruct((BLK, width)...  33.8 us
    pallas_call x1, Pallas kernels, gather(): pl.pallas_call(gather_kernel, out_shape=(jax.ShapeDtypeStruct((SIDE, widt...  29.5 us
    pallas_call x1, Pallas kernels, cell(): pl.pallas_call(cell_kernel, out_shape=(jax.ShapeDtypeStruct((SIDE, width)...  19.3 us

profile of v8, /device:TPU:1, one launch (start us, length us, event | category | flops | bytes accessed | tf_op | source)
XLA Modules:
  0.0 84.4 jit_solution(17833403707614485562)
XLA Ops:
  0.0 29.5 %gather_blocks.1 = (bf16[768,768]{1,0:T(8,128)(2,1)}, bf16[768,768]{1,0:T(8,128)(2,1)}, s32[256,1,128]{2,1,0:T(1,128)}) custom-call(bf16[192,1024]{1,0:T(8,128)(2,1)} %bitcast.5, bf16[1024,768]{1,0:T(8,128)(2,1)} %proj_hbm.1, s32[2,32]{1,0:T(2,128)} %bitcast.6, s32[1,32]{1,0:T(1,128)} %bitcast.7), custom_call_target="tpu_custom_call" | custom-call | tf_op jit(solution)/shard_map/gather_blocks/pallas_call | solution.py:287
  29.5 19.3 %cell_pairs.1 = (bf16[768,768]{1,0:T(8,128)(2,1)}, bf16[768,768]{1,0:T(8,128)(2,1)}) custom-call(f32[16]{0:T(128)} %table_ref.1, s32[256,1,128]{2,1,0:T(1,128)} %get-tuple-element.10.list_hbm, bf16[768,768]{1,0:T(8,128)(2,1)} %get-tuple-element.11.a_hbm, bf16[768,768]{1,0:T(8,128)(2,1)} %get-tuple-element.12.b_hbm, bf16[768,768]{1,0:T(8,128)(2,1)} %wq_hbm.1, ...), custom_call_target="tpu_custom_call" | custom-call | tf_op jit(solution)/shard_map/cell_pairs/pallas_call | solution.py:542
  48.9 33.8 %reduce_back.1 = bf16[192,768]{1,0:T(8,128)(2,1)} custom-call(bf16[768,768]{1,0:T(8,128)(2,1)} %get-tuple-element.13.pa_hbm, bf16[768,768]{1,0:T(8,128)(2,1)} %get-tuple-element.14.pb_hbm), custom_call_target="tpu_custom_call" | custom-call | tf_op jit(solution)/shard_map/reduce_back/pallas_call | solution.py:865
  82.7 1.7 %copy.12 = bf16[8,24,768]{2,1,0:T(8,128)(2,1)} copy(bf16[8,24,768]{2,1,0:T(8,128)(2,1)} %bitcast.4) | data formatting | bytes 589824

commit v9 on v8

--- a/solution.py
+++ b/solution.py
@@ -129,13 +129,6 @@
     list_out[row_me, :, 3 * PAIR_DEV :] = jnp.zeros((1, 128 - 3 * PAIR_DEV), jnp.int32)
     pl.semaphore_wait(barrier, n_peers + jnp.where(odd, 1, 0))
 
-    lz = []
-    for d in range(1, NZ):
-        mine = list_out.at[pl.ds(row_me, 1)]
-        cp = remote(mine, mine, lz_send.at[d], lz_recv.at[d], dev((z + d) % NZ, x, c, y))
-        cp.start()
-        lz.append(cp)
-
     s_b = (z // 4) * 2 + c
     b_dst = b_out.at[pl.ds(pl.multiple_of(s_b * BLK, BLK), BLK)]
     z0 = (z - y + NZ) % NZ
@@ -166,6 +159,13 @@
         @pl.when(go)
         def _(cp=cp):
             cp.start()
+
+    lz = []
+    for d in range(1, NZ):
+        mine = list_out.at[pl.ds(row_me, 1)]
+        cp = remote(mine, mine, lz_send.at[d], lz_recv.at[d], dev((z + d) % NZ, x, c, y))
+        cp.start()
+        lz.append(cp)
 
     for cp in lz:
         cp.wait_recv()

time: 84.8 us -> 96.8 us (1.14)
  Pallas kernels: 82.7 us -> 95 us
    pallas_call x1, Pallas kernels: 29.5 us -> 40.4 us  [gather(): pl.pallas_call(gather_kernel, out_shape=(jax.ShapeDtypeStruct((SIDE, widt...]
    pallas_call x1, Pallas kernels: 19.3 us -> 23.8 us  [cell(): pl.pallas_call(cell_kernel, out_shape=(jax.ShapeDtypeStruct((SIDE, width)...]
    pallas_call x1, Pallas kernels: 33.8 us -> 30.8 us  [reduce_back(): pl.pallas_call(reduce_kernel, out_shape=jax.ShapeDtypeStruct((BLK, width)...]
where the time goes in v9:
time: 96.8 us; the launch traced here: 96.7 us
  Pallas kernels  95 us (98%)
  local copies, waits for them, and re-layouts  1.69 us (2%)
    pallas_call x1, Pallas kernels, gather(): pl.pallas_call(gather_kernel, out_shape=(jax.ShapeDtypeStruct((SIDE, widt...  40.4 us
    pallas_call x1, Pallas kernels, reduce_back(): pl.pallas_call(reduce_kernel, out_shape=jax.ShapeDtypeStruct((BLK, width)...  30.8 us
    pallas_call x1, Pallas kernels, cell(): pl.pallas_call(cell_kernel, out_shape=(jax.ShapeDtypeStruct((SIDE, width)...  23.8 us

profile of v9, /device:TPU:1, one launch (start us, length us, event | category | flops | bytes accessed | tf_op | source)
XLA Modules:
  0.0 96.7 jit_solution(6539441674199180896)
XLA Ops:
  0.0 40.4 %gather_blocks.1 = (bf16[768,768]{1,0:T(8,128)(2,1)}, bf16[768,768]{1,0:T(8,128)(2,1)}, s32[256,1,128]{2,1,0:T(1,128)}) custom-call(bf16[192,1024]{1,0:T(8,128)(2,1)} %bitcast.5, bf16[1024,768]{1,0:T(8,128)(2,1)} %proj_hbm.1, s32[2,32]{1,0:T(2,128)} %bitcast.6, s32[1,32]{1,0:T(1,128)} %bitcast.7), custom_call_target="tpu_custom_call" | custom-call | tf_op jit(solution)/shard_map/gather_blocks/pallas_call | solution.py:287
  40.4 23.8 %cell_pairs.1 = (bf16[768,768]{1,0:T(8,128)(2,1)}, bf16[768,768]{1,0:T(8,128)(2,1)}) custom-call(f32[16]{0:T(128)} %table_ref.1, s32[256,1,128]{2,1,0:T(1,128)} %get-tuple-element.10.list_hbm, bf16[768,768]{1,0:T(8,128)(2,1)} %get-tuple-element.11.a_hbm, bf16[768,768]{1,0:T(8,128)(2,1)} %get-tuple-element.12.b_hbm, bf16[768,768]{1,0:T(8,128)(2,1)} %wq_hbm.1, ...), custom_call_target="tpu_custom_call" | custom-call | tf_op jit(solution)/shard_map/cell_pairs/pallas_call | solution.py:542
  64.2 30.8 %reduce_back.1 = bf16[192,768]{1,0:T(8,128)(2,1)} custom-call(bf16[768,768]{1,0:T(8,128)(2,1)} %get-tuple-element.13.pa_hbm, bf16[768,768]{1,0:T(8,128)(2,1)} %get-tuple-element.14.pb_hbm), custom_call_target="tpu_custom_call" | custom-call | tf_op jit(solution)/shard_map/reduce_back/pallas_call | solution.py:865
  95.1 1.7 %copy.12 = bf16[8,24,768]{2,1,0:T(8,128)(2,1)} copy(bf16[8,24,768]{2,1,0:T(8,128)(2,1)} %bitcast.4) | data formatting | bytes 589824
